TPU v7x, 32 devices: a whole 2x2x4 slice. The times are simulated.
32 devices in a mesh: doc: 4 (over y, x), term: 4 (over z), pair: 2 (over core).
Axes of the slice: x: 2, y: 2, z: 4, core: 2. Of those that a mesh axis runs over, the one named last changes fastest.
Arguments:
- counts: int32 [8, 16, 128, 128], P('doc', 'term'), may hold values from 0 to 11
- block_ids: int32 [8, 16], P('doc', 'term'), may hold values from 0 to 8191, as said below
- live_slots: int32 [8, 16], P('doc', 'term'), may hold values 0 or 1
- lengths: int32 [1024], P('doc'), may hold values from 1 to 24528, as said below
- pairs: int32 [512, 2], P(('doc', 'pair')), may hold values from 0 to 7, as said below
- pair_count: int32 [8], P(('doc', 'pair')), may hold values from 1 to 64, as said below
Outputs:
- gram: float32 [512, 128, 128], P(('doc', 'pair'), 'term')
Inputs may be any that keep to these rules, and one draw needn't show every extreme that they name: `block_ids`: columns s * 4 to (s + 1) * 4 - 1 hold term blocks of the s-th of 4 equal ranges of the 8192 blocks, distinct within one document block and range. `lengths`: document b * 128 + r has a length of the sum of counts[b, s, r, t] over all slots s and all t plus tokens outside its blocks: 1 to 2000 of them for every document but the last, whose length is exactly 24528. `pairs`: the left block of row k belongs to doc index k // 128. Rows k with k % 64 < pair_count[k // 64] are live; some entry equals 64.
All inputs are finite; a program needn't handle non-finite values. No bound on the sum of `live_slots` on one device may be relied on, other than what follows from the above.
Results may differ from a plain program's by a relative error of at most 0.0014.
Values may be sent and summed in bfloat16 or wider, within the bound.
A program may use at most 64 MiB of HBM per device.

v0:
```python
import jax
import jax.numpy as jnp
from jax import lax
from jax.sharding import PartitionSpec as P

V = 1048576
PB = 8


saturation = 1.2
length_weight = 0.75
epsilon = 1e-06


def partner(block, axis, stride):
    count = lax.axis_size(axis)
    route = []
    for low in range(count):
        high = low | 1 << stride
        if high != low and high < count:
            route += [(low, high), (high, low)]
    return lax.ppermute(block, axis, route)


def gram_block(normalized, block_ids, whole_tiles, whole_ids, pair_batch, left_base):
    left_index = pair_batch[:, 0] - left_base
    right_pair_index = pair_batch[:, 1]
    left_tiles = normalized[left_index]
    right_tiles = whole_tiles[right_pair_index]
    matches = (block_ids[left_index][:, :, None] == whole_ids[right_pair_index][:, None, :]).astype(
        jnp.bfloat16
    )
    aligned = jnp.einsum(
        "pij,pjet->piet", matches, right_tiles, preferred_element_type=jnp.float32
    ).astype(jnp.bfloat16)
    return jnp.einsum("pidt,piet->pde", left_tiles, aligned, preferred_element_type=jnp.float32)


def run_pairs(work_pairs, work_count, normalized, block_ids, whole_tiles, whole_ids, left_base):
    capacity = work_pairs.shape[0]
    doc_rows = normalized.shape[2]
    step_count = (work_count + PB - 1) // PB

    def pair_step(loop_index, partial_value):
        first_row = loop_index * PB
        pair_batch = lax.dynamic_slice_in_dim(work_pairs, first_row, PB, 0)
        gram_tiles = gram_block(
            normalized, block_ids, whole_tiles, whole_ids, pair_batch, left_base
        )
        live_mask = first_row + jnp.arange(PB, dtype=jnp.int32) < work_count
        gram_tiles = jnp.where(live_mask[:, None, None], gram_tiles, 0.0)
        return lax.dynamic_update_slice_in_dim(partial_value, gram_tiles, first_row, 0)

    return lax.fori_loop(
        0, step_count, pair_step, jnp.zeros((capacity, doc_rows, doc_rows), jnp.float32)
    )


def shards(counts, block_ids, live_slots, lengths, pairs, pair_count):
    block_count, slot_count, doc_rows, term_columns = counts.shape
    covered_blocks = V // term_columns // lax.axis_size("term")
    local_ids = block_ids - lax.axis_index("term") * covered_blocks
    present = (counts > 0) & (live_slots[:, :, None, None] > 0)
    col_docs = jnp.sum(present.astype(jnp.float32), axis=2)
    freq_part = (
        jnp.zeros((covered_blocks, term_columns), jnp.float32)
        .at[local_ids.reshape(-1)]
        .add(col_docs.reshape(-1, term_columns))
    )
    len_float = lengths.astype(jnp.float32)
    doc_freq, len_total = (
        lax.psum(freq_part.astype(jnp.bfloat16), "doc").astype(jnp.float32),
        lax.psum(jnp.sum(len_float).astype(jnp.bfloat16), "doc").astype(jnp.float32),
    )
    docs_all = len_float.shape[0] * lax.axis_size("doc")
    avg_len = len_total / docs_all
    inv_freq = jnp.log(1.0 + (docs_all - doc_freq + 0.5) / (doc_freq + 0.5))
    slot_freq = inv_freq[local_ids]
    len_scale = (
        1.0
        - length_weight
        + length_weight * len_float.reshape(block_count, 1, doc_rows, 1) / avg_len
    )
    term_freq = counts.astype(jnp.float32)
    weight = jnp.where(
        present,
        slot_freq[:, :, None, :]
        * term_freq
        * (saturation + 1.0)
        / (term_freq + saturation * len_scale),
        0.0,
    )
    square_sum = lax.psum(jnp.sum(weight * weight, axis=(1, 3)), "term")
    normalized = (weight * lax.rsqrt(square_sum + epsilon)[:, None, :, None]).astype(jnp.bfloat16)
    whole_tiles, whole_ids = (
        lax.all_gather(normalized, "doc", axis=0, tiled=True),
        lax.all_gather(block_ids, "doc", axis=0, tiled=True),
    )
    left_base = lax.axis_index("doc") * block_count
    own_count = pair_count[0]
    capacity = pairs.shape[0]
    other_pairs, other_count = partner((pairs, pair_count), "pair", 0)
    pair_side = lax.axis_index("pair")
    first_pairs = jnp.where(pair_side == 0, pairs, other_pairs)
    second_pairs = jnp.where(pair_side == 0, other_pairs, pairs)
    first_count = jnp.where(pair_side == 0, own_count, other_count[0])
    second_count = jnp.where(pair_side == 0, other_count[0], own_count)
    total_pairs = first_count + second_count
    half_work = (total_pairs + 1) // 2
    work_count = jnp.where(pair_side == 0, half_work, total_pairs - half_work)
    combined = pair_side * half_work + jnp.arange(capacity, dtype=jnp.int32)
    from_first = jnp.take(first_pairs, jnp.clip(combined, 0, capacity - 1), axis=0)
    from_second = jnp.take(second_pairs, jnp.clip(combined - first_count, 0, capacity - 1), axis=0)
    work_pairs = jnp.where((combined < first_count)[:, None], from_first, from_second)
    partial_value = run_pairs(
        work_pairs, work_count, normalized, block_ids, whole_tiles, whole_ids, left_base
    )
    own_grams = lax.psum_scatter(partial_value, "term", scatter_dimension=1, tiled=True)
    other_grams = partner(own_grams, "pair", 0)
    slot_index = jnp.arange(capacity, dtype=jnp.int32)
    placed = slot_index + pair_side * first_count
    holder = placed // half_work
    within = jnp.clip(placed - holder * half_work, 0, capacity - 1)
    picked_own = jnp.take(own_grams, within, axis=0)
    picked_other = jnp.take(other_grams, within, axis=0)
    merged = jnp.where((holder == pair_side)[:, None, None], picked_own, picked_other)
    return jnp.where((slot_index < own_count)[:, None, None], merged, 0.0)


def solution(mesh):
    in_specs = (
        P("doc", "term", None, None),
        P("doc", "term"),
        P("doc", "term"),
        P("doc"),
        P(("doc", "pair"), None),
        P(("doc", "pair")),
    )
    out_specs = P(("doc", "pair"), "term", None)
    return jax.shard_map(shards, mesh=mesh, in_specs=in_specs, out_specs=out_specs, check_vma=False)
```

profile of v0, /device:TPU:0, one launch (start us, length us, event | category | flops | bytes accessed | tf_op | source)
XLA Modules:
  0.0 213.7 jit_solution(9668799092709207815)
XLA Ops:
  6.5 0.7 compare_select_fusion.2
  7.4 0.7 broadcast_compare_fusion
  8.1 1.2 convert_reduce_fusion
  9.3 0.9 scatter_custom_fusion
  10.1 0.8 convert_element_type.29
  11.1 1.4 convert_reduce_fusion.1
  12.4 12.1 %psum.22 = bf16[]{:T(256)} all-reduce(bf16[]{:T(256)} %convert_reduce_fusion.1), channel_id=1, replica_groups=mesh['doc'=4,'term'=4,'pair'=2] {'doc'}, use_global_device_ids=true, to_apply=%region_4.6 | all-reduce | flops 1 | bytes 4 | tf_op jit(solution)/shard_map/psum | solution.py:73
  25.3 0.7 multiply_bitcast_fusion
  26.0 33.2 %all-reduce.2.cloned.1.call-done = bf16[2048,128]{1,0:T(8,128)(2,1)} async-done(((bf16[2048,128]{1,0:T(8,128)(2,1)}), bf16[2048,128]{1,0:T(8,128)(2,1)}) %all-reduce.2.cloned.1.call-update) | async-done | bytes 524304 | tf_op jit(solution)/shard_map/psum | solution.py:72
  59.2 1.3 fusion.12
  60.5 0.6 gather_fusion.4
  61.5 11.7 %psum.23 = f32[2,128]{1,0:T(2,128)S(1)} all-reduce(f32[2,128]{1,0:T(2,128)S(1)} %multiply_reduce_fusion), channel_id=1, replica_groups=mesh['doc'=4,'term'=4,'pair'=2] {'term'}, use_global_device_ids=true, to_apply=%region_6.0 | all-reduce | flops 256 | bytes 2048 | tf_op jit(solution)/shard_map/psum | solution.py:93
  73.2 1.0 multiply_convert_fusion
  75.0 8.0 %all-gather = s32[4,2,4]{2,1,0:T(2,128)S(1)} all-gather(s32[1,2,4]{2,1,0:T(2,128)S(1)} %bitcast.38), channel_id=1, replica_groups=mesh['doc'=4,'term'=4,'pair'=2] {'doc'}, dimensions={0}, use_global_device_ids=true | all-gather | bytes 160 | tf_op jit(solution)/shard_map/all_gather | solution.py:97
  85.1 0.6 gather_fusion.6
  85.7 0.6 gather_fusion.5
  86.4 11.9 %all-gather.3.cloned.1.call-done = bf16[8,4,128,128]{3,2,1,0:T(8,128)(2,1)} async-done(((bf16[2,4,128,128]{3,2,1,0:T(8,128)(2,1)}), bf16[8,4,128,128]{3,2,1,0:T(8,128)(2,1)}) %all-gather.3.cloned.1.call-update) | async-done | bytes 1048592 | tf_op jit(solution)/shard_map/all_gather | solution.py:96
  98.3 2.4 %broadcast_in_dim.87 = f32[64,128,128]{2,1,0:T(8,128)} broadcast(f32[]{:T(128)} %constant.64.clone.1), dimensions={} | broadcast | bytes 4194308 | tf_op jit(solution)/shard_map/broadcast_in_dim | solution.py:55
  100.7 24.8 %while.10 = (s32[]{:T(128)}, f32[64,128,128]{2,1,0:T(8,128)}, s32[]{:T(128)}, s32[]{:T(128)}, s32[64,2]{0,1:T(2,128)S(1)}, /*index=5*/s32[]{:T(128)}, bf16[2,4,1...) while((s32[]{:T(128)}, f32[64,128,128]{2,1,0:T(8,128)}, ...), condition=%wide.region_8.10_spmd, body=%wide.region_7.9_spmd.sunk | while | flops 139069648 | bytes 8922519 | solution.py:54
  100.8 0.7 gather_fusion.1
  101.6 0.6 gather_fusion.2
  102.1 0.6 gather_fusion.3
  102.7 1.0 convolution_convert_fusion.2
  103.7 0.7 gather_fusion
  104.4 1.2 fusion.30
  105.8 0.7 gather_fusion.1
  106.5 0.6 gather_fusion.2
  107.6 1.0 convolution_convert_fusion.2
  108.6 0.7 gather_fusion
  109.4 1.2 fusion.30
  110.7 0.7 gather_fusion.1
  112.0 0.6 gather_fusion.3
  112.6 1.0 convolution_convert_fusion.2
  113.6 0.7 gather_fusion
  114.3 1.3 fusion.30
  115.7 0.7 gather_fusion.1
  117.6 1.0 convolution_convert_fusion.2
  118.5 0.7 gather_fusion
  119.3 1.3 fusion.30
  120.6 0.7 gather_fusion.1
  122.5 1.0 convolution_convert_fusion.2
  123.5 0.7 gather_fusion
  124.3 1.2 fusion.30
  125.5 76.9 %reduce-scatter.2.cloned.1.call-done = f32[64,32,128]{2,1,0:T(8,128)} async-done(((f32[64,128,128]{2,1,0:T(8,128)}), f32[64,32,128]{2,1,0:T(8,128)}) %reduce-scatter.2.cloned.1.call-update) | async-done | bytes 1048592 | tf_op jit(solution)/shard_map/reduce_scatter | solution.py:118
  202.6 1.8 gather_fusion.7
  204.4 0.9 collective-permute-done.2
  205.3 0.6 gather_fusion.8
  205.9 1.2 fusion.13
  (65 shorter events, 5.6 us)
Async XLA Ops:
  6.5 68.5 %copy-start.1 = (s32[2,4]{1,0:T(2,128)S(1)}, s32[2,4]{1,0:T(2,128)}, u32[]{:S(2)}) copy-start(s32[2,4]{1,0:T(2,128)} %param.13) | copy-start | bytes 100
  6.5 54.6 %copy-start.3 = (s32[2,4,128,128]{3,2,1,0:T(8,128)S(1)}, s32[2,4,128,128]{3,2,1,0:T(8,128)}, u32[]{:S(2)}) copy-start(s32[2,4,128,128]{3,2,1,0:T(8,128)} %param.12) | copy-start | bytes 1572868
  6.5 67.9 %copy-start.4 = (s32[64,2]{0,1:T(2,128)S(1)}, s32[64,2]{0,1:T(2,128)}, u32[]{:S(2)}) copy-start(s32[64,2]{0,1:T(2,128)} %param.16) | copy-start | bytes 1540
  6.5 52.7 %all-reduce.2.cloned.1.call-start = ((), (), s32[]{:S(2)}) async-start(), calls=%async_computation.1 | async-start | bytes 1048576 | tf_op jit(solution)/shard_map/psum | solution.py:72
  11.0 87.3 %all-gather.3.cloned.1.call-start = ((), (), s32[]{:S(2)}) async-start(), calls=%async_computation.2 | async-start | bytes 1310720 | tf_op jit(solution)/shard_map/all_gather | solution.py:96
  74.2 26.5 %copy-start = (bf16[2,4,128,128]{3,2,1,0:T(8,128)(2,1)S(1)}, bf16[2,4,128,128]{3,2,1,0:T(8,128)(2,1)}, u32[]{:S(2)}) copy-start(bf16[2,4,128,128]{3,2,1,0:T(8,128)(2,1)} %multiply_convert_fusion) | copy-start | bytes 786436
  74.3 128.2 %reduce-scatter.2.cloned.1.call-start = ((), (), s32[]{:S(2)}) async-start(), calls=%async_computation.3 | async-start | bytes 5242880 | tf_op jit(solution)/shard_map/reduce_scatter | solution.py:118
  74.3 9.4 %collective-permute-start = (s32[1]{0:T(128)}, s32[1]{0:T(128)}, u32[]{:S(2)}, u32[]{:S(2)}) collective-permute-start(s32[1]{0:T(128)} %param.17), channel_id=1, source_target_pairs={{0,1},{1,0},{2,3},{3,2},{4,5},{5,4},{6,7},{7,6},{8,9},{9,8},{10,11... | collective-permute-start | bytes 20 | tf_op jit(solution)/shard_map/ppermute | solution.py:22
  74.5 10.5 %collective-permute-start.1 = (s32[64,2]{1,0:T(8,128)S(1)}, s32[64,2]{1,0:T(8,128)S(1)}, u32[]{:S(2)}, u32[]{:S(2)}) collective-permute-start(s32[64,2]{1,0:T(8,128)S(1)} %copy.18), channel_id=1, source_target_pairs={{0,1},{1,0},{2,3},{3,2},{4,5},{5,4},{6,7},{7,6},{8,9},{9,8},{10,11... | collective-permute-start | bytes 1544 | tf_op jit(solution)/shard_map/ppermute | solution.py:22
  98.3 2.5 %copy-start.2 = (bf16[8,4,128,128]{3,2,1,0:T(8,128)(2,1)S(1)}, bf16[8,4,128,128]{3,2,1,0:T(8,128)(2,1)}, u32[]{:S(2)}) copy-start(bf16[8,4,128,128]{3,2,1,0:T(8,128)(2,1)} %all-gather.3.cloned.1.call-done) | copy-start | bytes 3145732
  202.4 2.9 %collective-permute-start.2 = (f32[64,32,128]{2,1,0:T(8,128)}, f32[64,32,128]{2,1,0:T(8,128)S(1)}, u32[]{:S(2)}, u32[]{:S(2)}) collective-permute-start(f32[64,32,128]{2,1,0:T(8,128)} %reduce-scatter.2.cloned.1.call-done), channel_id=1, source_target_pairs={{0,1},{1,0},{2,3},{3,2},{4,5},{5,4},{6,7},{7,6},{8,9},{9,8},{10,11... | collective-permute-start | bytes 3145736 | tf_op jit(solution)/shard_map/ppermute | solution.py:22
Sparse Core Ops, SparseCore 0:
  11.1 48.0 all-reduce.1
  74.4 23.8 all-gather.2
  125.7 76.7 reduce-scatter.1
where the time goes:
time: 214 us
  waiting for transfers between devices  123 us (57%)
  blocking collectives  31.8 us (15%)
  local copies, waits for them, and re-layouts  20.4 us (10%)
  between operations  15.8 us (7%)
  matrix products  11.1 us (5%)
  other arithmetic  10.8 us (5%)
    reduce_scatter x1, waiting for transfers between devices, shards(): lax.psum_scatter(partial_value, 'term', scatter_dimension=1, tiled=True)  76.9 us
    psum x1, waiting for transfers between devices, shards(): lax.psum(freq_part.astype(jnp.bfloat16), 'doc').astype(jnp.float32)  33.2 us
    psum x1, blocking collectives, shards(): lax.psum(jnp.sum(len_float).astype(jnp.bfloat16), 'doc').astype(jnp.float32)  12.1 us
    all_gather x1, waiting for transfers between devices, shards(): lax.all_gather(normalized, 'doc', axis=0, tiled=True)  11.9 us
    psum x1, blocking collectives, shards(): square_sum = lax.psum(jnp.sum(weight * weight, axis=(1, 3)), 'term')  11.7 us
    all_gather x1, blocking collectives, shards(): lax.all_gather(block_ids, 'doc', axis=0, tiled=True)  7.99 us
    dot_general x5, matrix products, gram_block(): jnp.einsum('pidt,piet->pde', left_tiles, aligned, preferred_element_type=...  6.22 us
    dot_general x5, matrix products, gram_block(): jnp.einsum('pij,pjet->piet', matches, right_tiles, preferred_element_type...  4.85 us
  transfers between devices with their start and end apart: 6, of which 4 were waited for; matrix products, arithmetic and copies ran while one was open for 3% of the time, Pallas kernels for 0%

commit v1 on v0

v1 whole, which is shorter than its diff:
```python
import functools

import jax
import jax.numpy as jnp
from jax import lax
from jax.experimental import pallas as pl
from jax.experimental.pallas import tpu as pltpu
from jax.sharding import PartitionSpec as P

saturation = 1.2
length_weight = 0.75
epsilon = 1e-06

MESH = pl.DeviceIdType.MESH


def tiles_kernel(
    sizes,
    live_ref,
    ids_ref,
    counts_ref,
    lengths_ref,
    out_ref,
    masked,
    small,
    right_counts,
    left_weight,
    right_weight,
    partial_sum,
    term_recv,
    square_own,
    square_recv,
    column,
    final,
    pair_recv,
    small_send_sem,
    small_recv_sem,
    count_send_sem,
    count_recv_sem,
    term_send_sem,
    term_recv_sem,
    square_send_sem,
    square_recv_sem,
    pair_send_sem,
    pair_recv_sem,
):
    n_doc, n_term, n_pair = sizes
    blocks, slots, rows, cols = counts_ref.shape
    per_core = blocks // n_pair
    n_right = n_doc * per_core
    part_rows = rows // n_term
    docs_all = n_doc * blocks * rows
    me_doc = lax.axis_index("doc")
    me_term = lax.axis_index("term")
    me_pair = lax.axis_index("pair")

    def doc_peer(k):
        return {"doc": lax.rem(me_doc + k, n_doc)}

    def term_peer(k):
        return {"term": lax.rem(me_term + k, n_term)}

    def pair_peer(k):
        return {"pair": lax.rem(me_pair + k, n_pair)}

    def small_copy(k):
        return pltpu.make_async_remote_copy(
            src_ref=small.at[0],
            dst_ref=small.at[k],
            send_sem=small_send_sem.at[k],
            recv_sem=small_recv_sem.at[k],
            device_id=doc_peer(k),
            device_id_type=MESH,
        )

    def count_copy(k):
        return pltpu.make_async_remote_copy(
            src_ref=masked.at[pl.ds(me_pair * per_core, per_core)],
            dst_ref=right_counts.at[k],
            send_sem=count_send_sem.at[k],
            recv_sem=count_recv_sem.at[k],
            device_id=doc_peer(k),
            device_id_type=MESH,
        )

    def term_copy(m, k):
        return pltpu.make_async_remote_copy(
            src_ref=partial_sum.at[m, lax.rem(me_term + k, n_term)],
            dst_ref=term_recv.at[m, k],
            send_sem=term_send_sem.at[m, k],
            recv_sem=term_recv_sem.at[m, k],
            device_id=term_peer(k),
            device_id_type=MESH,
        )

    def square_copy(k):
        return pltpu.make_async_remote_copy(
            src_ref=square_own,
            dst_ref=square_recv.at[k],
            send_sem=square_send_sem.at[k],
            recv_sem=square_recv_sem.at[k],
            device_id=term_peer(k),
            device_id_type=MESH,
        )

    def pair_copy(m, k):
        return pltpu.make_async_remote_copy(
            src_ref=final.at[m],
            dst_ref=pair_recv.at[k, m],
            send_sem=pair_send_sem.at[m, k],
            recv_sem=pair_recv_sem.at[m, k],
            device_id=pair_peer(k),
            device_id_type=MESH,
        )

    barrier = pltpu.get_barrier_semaphore()
    for k in range(1, n_doc):
        pl.semaphore_signal(barrier, inc=1, device_id=doc_peer(k), device_id_type=MESH)
    for k in range(1, n_term):
        pl.semaphore_signal(barrier, inc=1, device_id=term_peer(k), device_id_type=MESH)
    for k in range(1, n_pair):
        pl.semaphore_signal(barrier, inc=1, device_id=pair_peer(k), device_id_type=MESH)

    small[0] = jnp.zeros(small.shape[1:], jnp.float32)
    for b in range(blocks):
        for s in range(slots):
            live = jnp.full((rows, cols), live_ref[b, s], jnp.int32) > 0
            value = jnp.where(live, counts_ref[b, s].astype(jnp.float32), 0.0)
            masked[b, s] = value.astype(jnp.bfloat16)
            small[0, b, s : s + 1] = jnp.sum(
                jnp.where(value > 0.0, 1.0, 0.0), axis=0, keepdims=True
            )
            small[0, b, slots + s : slots + s + 1] = jnp.full(
                (1, cols), ids_ref[b, s], jnp.int32
            ).astype(jnp.float32)
    small[0, blocks, 0:blocks] = lengths_ref[...].astype(jnp.float32)
    square_own[...] = jnp.zeros(square_own.shape, jnp.float32)

    pl.semaphore_wait(barrier, n_doc + n_term + n_pair - 3)

    for k in range(1, n_doc):
        small_copy(k).start()
    for k in range(1, n_doc):
        count_copy(k).start()
    for k in range(1, n_doc):
        small_copy(k).wait_recv()

    total_len = lax.fori_loop(
        0,
        n_doc,
        lambda k, acc: acc + jnp.sum(small[k, blocks], axis=0, keepdims=True),
        jnp.zeros((1, cols), jnp.float32),
    )
    avg_len = jnp.sum(total_len, axis=1, keepdims=True) / docs_all

    def inv_freq_of(ids):
        def add(k, acc):
            for b in range(blocks):
                table = small[k, b]
                for s in range(slots):
                    same = ids == table[slots + s : slots + s + 1]
                    acc = acc + jnp.where(same, table[s : s + 1], 0.0)
            return acc

        freq = lax.fori_loop(0, n_doc, add, jnp.zeros(ids.shape, jnp.float32))
        return jnp.log(1.0 + (docs_all - freq + 0.5) / (freq + 0.5))

    def weigh(k, b, read, target, square_row):
        inv_freq = inv_freq_of(small[k, b, slots : 2 * slots]) * (saturation + 1.0)
        length = small[k, blocks, pl.ds(b, 1)]
        scale = saturation * (1.0 - length_weight + length_weight * length / avg_len)
        scale = jnp.transpose(jnp.broadcast_to(scale, (rows, rows)))
        squares = jnp.zeros((rows, cols), jnp.float32)
        for s in range(slots):
            freq = read(s).astype(jnp.float32)
            weight = inv_freq[s : s + 1] * freq / (freq + scale)
            squares = squares + weight * weight
            target[s] = weight.astype(jnp.bfloat16)
        square_own[pl.ds(square_row, 1)] = jnp.sum(
            jnp.transpose(squares), axis=0, keepdims=True
        )

    for b in range(blocks):
        weigh(0, b, lambda s, b=b: masked[b, s], left_weight.at[b], b)

    def grams(m, right, right_ids):
        for b in range(blocks):
            left_ids = small[0, b, slots : 2 * slots]
            gram = jnp.zeros((rows, rows), jnp.float32)
            for i in range(slots):
                aligned = jnp.zeros((rows, cols), jnp.bfloat16)
                for j in range(slots):
                    same = left_ids[i : i + 1] == right_ids[j : j + 1]
                    same = jnp.where(same, 1.0, 0.0).astype(jnp.bfloat16)
                    aligned = aligned + right[j] * same
                gram = gram + lax.dot_general(
                    left_weight[b, i],
                    aligned,
                    (((1,), (1,)), ((), ())),
                    preferred_element_type=jnp.float32,
                )
            for z in range(n_term):
                partial_sum[m, z, b] = gram[z * part_rows : (z + 1) * part_rows]
        for k in range(1, n_term):
            term_copy(m, k).start()

    for i in range(per_core):
        own = me_pair * per_core + i
        square_own[pl.ds(blocks + i, 1)] = square_own[pl.ds(own, 1)]
        grams(i, left_weight.at[own], small[0, own, slots : 2 * slots])

    def right_step(k, carry):
        count_copy(k).wait_recv()
        for i in range(per_core):
            b = me_pair * per_core + i
            m = k * per_core + i
            weigh(k, b, lambda s, i=i: right_counts[k, i, s], right_weight, blocks + m)

            @pl.when(m == n_right - 1)
            def _():
                for t in range(1, n_term):
                    square_copy(t).start()

            grams(m, right_weight, small[k, b, slots : 2 * slots])
        return carry

    lax.fori_loop(1, n_doc, right_step, 0)

    squares = square_own[...]
    for k in range(1, n_term):
        square_copy(k).wait_recv()
        squares = squares + square_recv[k]
    inverse = lax.rsqrt(squares + epsilon)
    square_own_done = [square_copy(k) for k in range(1, n_term)]
    for copy in square_own_done:
        copy.wait_send()
    square_own[...] = inverse
    left_scale = []
    for b in range(blocks):
        column[...] = jnp.transpose(jnp.broadcast_to(inverse[b : b + 1], (rows, rows)))
        left_scale.append(column[pl.ds(me_term * part_rows, part_rows)])

    def finish(m, carry):
        for k in range(1, n_term):
            term_copy(m, k).wait_recv()
        right_scale = square_own[pl.ds(blocks + m, 1)]
        for b in range(blocks):
            total = partial_sum[m, me_term, b]
            for k in range(1, n_term):
                total = total + term_recv[m, k, b]
            value = total * left_scale[b] * right_scale
            final[m, b] = value
            out_ref[0, m, b] = value
        for k in range(1, n_pair):
            pair_copy(m, k).start()
        return carry

    lax.fori_loop(0, n_right, finish, 0)

    def collect(m, carry):
        for k in range(1, n_pair):
            pair_copy(m, k).wait_recv()
            out_ref[k, m] = pair_recv[k, m]
        for k in range(1, n_term):
            term_copy(m, k).wait_send()
        for k in range(1, n_pair):
            pair_copy(m, k).wait_send()
        return carry

    lax.fori_loop(0, n_right, collect, 0)
    for k in range(1, n_doc):
        small_copy(k).wait_send()
        count_copy(k).wait_send()


def place_kernel(sizes, blocks, pairs_ref, count_ref, tiles_ref, out_ref):
    n_doc, n_term, n_pair = sizes
    per_core = blocks // n_pair
    me_doc = lax.axis_index("doc")
    me_pair = lax.axis_index("pair")
    count = count_ref[0]

    def step(row, carry):
        live = row < count

        @pl.when(live)
        def _():
            left = pairs_ref[0, row] - me_doc * blocks
            right = pairs_ref[1, row]
            owner, inner = right // blocks, right % blocks
            side = lax.rem(me_pair - inner // per_core + n_pair, n_pair)
            m = lax.rem(me_doc - owner + n_doc, n_doc) * per_core + inner % per_core
            out_ref[row] = tiles_ref[side, m, left]

        @pl.when(jnp.logical_not(live))
        def _():
            out_ref[row] = jnp.zeros(out_ref.shape[1:], jnp.float32)

        return carry

    lax.fori_loop(0, out_ref.shape[0], step, 0, unroll=4)


def shards(sizes, counts, block_ids, live_slots, lengths, pairs, pair_count):
    n_doc, n_term, n_pair = sizes
    blocks, slots, rows, cols = counts.shape
    per_core = blocks // n_pair
    n_right = n_doc * per_core
    part_rows = rows // n_term
    table_rows = -(-max(2 * slots, blocks) // 8) * 8
    square_rows = -(-(blocks + n_right) // 8) * 8
    dma = pltpu.SemaphoreType.DMA
    smem = pl.BlockSpec(memory_space=pltpu.SMEM)
    vmem = pl.BlockSpec(memory_space=pltpu.VMEM)
    tiles = pl.pallas_call(
        functools.partial(tiles_kernel, sizes),
        out_shape=jax.ShapeDtypeStruct((n_pair, n_right, blocks, part_rows, rows), jnp.float32),
        in_specs=[smem, smem, vmem, vmem],
        out_specs=vmem,
        scratch_shapes=[
            pltpu.VMEM((blocks, slots, rows, cols), jnp.bfloat16),
            pltpu.VMEM((n_doc, blocks + 1, table_rows, cols), jnp.float32),
            pltpu.VMEM((n_doc, per_core, slots, rows, cols), jnp.bfloat16),
            pltpu.VMEM((blocks, slots, rows, cols), jnp.bfloat16),
            pltpu.VMEM((slots, rows, cols), jnp.bfloat16),
            pltpu.VMEM((n_right, n_term, blocks, part_rows, rows), jnp.float32),
            pltpu.VMEM((n_right, n_term, blocks, part_rows, rows), jnp.float32),
            pltpu.VMEM((square_rows, rows), jnp.float32),
            pltpu.VMEM((n_term, square_rows, rows), jnp.float32),
            pltpu.VMEM((rows, rows), jnp.float32),
            pltpu.VMEM((n_right, blocks, part_rows, rows), jnp.float32),
            pltpu.VMEM((n_pair, n_right, blocks, part_rows, rows), jnp.float32),
            dma((n_doc,)),
            dma((n_doc,)),
            dma((n_doc,)),
            dma((n_doc,)),
            dma((n_right, n_term)),
            dma((n_right, n_term)),
            dma((n_term,)),
            dma((n_term,)),
            dma((n_right, n_pair)),
            dma((n_right, n_pair)),
        ],
        compiler_params=pltpu.CompilerParams(
            collective_id=0, has_side_effects=True, vmem_limit_bytes=48 * 1024 * 1024
        ),
    )(live_slots, block_ids, counts, lengths.reshape(blocks, rows))
    return pl.pallas_call(
        functools.partial(place_kernel, sizes, blocks),
        out_shape=jax.ShapeDtypeStruct((pairs.shape[0], part_rows, rows), jnp.float32),
        in_specs=[smem, smem, vmem],
        out_specs=vmem,
        compiler_params=pltpu.CompilerParams(vmem_limit_bytes=48 * 1024 * 1024),
    )(pairs.T, pair_count, tiles)


def solution(mesh):
    sizes = (mesh.shape["doc"], mesh.shape["term"], mesh.shape["pair"])
    in_specs = (
        P("doc", "term", None, None),
        P("doc", "term"),
        P("doc", "term"),
        P("doc"),
        P(("doc", "pair"), None),
        P(("doc", "pair")),
    )
    out_specs = P(("doc", "pair"), "term", None)
    return jax.shard_map(
        functools.partial(shards, sizes),
        mesh=mesh,
        in_specs=in_specs,
        out_specs=out_specs,
        check_vma=False,
    )
```

time: 214 us -> 30.3 us (0.14)
  waiting for transfers between devices: 123 us -> 0 us
  blocking collectives: 31.8 us -> 0 us
  Pallas kernels: 0 us -> 27.7 us
  local copies, waits for them, and re-layouts: 20.4 us -> 1.73 us
  between operations: 15.8 us -> 0.7 us
  matrix products: 11.1 us -> 0 us
  other arithmetic: 10.8 us -> 0 us
    reduce_scatter x1 -> x0, waiting for transfers between devices: 76.9 us -> none  [shards(): lax.psum_scatter(partial_value, 'term', scatter_dimension=1, tiled=True)]
    psum x1 -> x0, waiting for transfers between devices: 33.2 us -> none  [shards(): lax.psum(freq_part.astype(jnp.bfloat16), 'doc').astype(jnp.float32)]
    pallas_call x0 -> x2, Pallas kernels: none -> 27.7 us  [the longest x1 24.4 us: shards(): pl.pallas_call(functools.partial(tiles_kernel, sizes), out_shape=jax.Shap...]
    psum x2 -> x0, blocking collectives: 23.8 us -> none  [the longest x1 12.1 us: shards(): lax.psum(jnp.sum(len_float).astype(jnp.bfloat16), 'doc').astype(jnp.float32)]
    gather x25 -> x0, local copies, waits for them, and re-layouts: 17.3 us -> none  [the longest x5 3.75 us: gram_block(): right_tiles = whole_tiles[right_pair_index]]
    all_gather x1 -> x0, waiting for transfers between devices: 11.9 us -> none  [shards(): lax.all_gather(normalized, 'doc', axis=0, tiled=True)]
    dot_general x10 -> x0, matrix products: 11.1 us -> none  [the longest x5 6.22 us: gram_block(): jnp.einsum('pidt,piet->pde', left_tiles, aligned, preferred_element_type=...]
    all_gather x1 -> x0, blocking collectives: 7.99 us -> none  [shards(): lax.all_gather(block_ids, 'doc', axis=0, tiled=True)]
  transfers between devices with their start and end apart: 6 -> 0, of which waited for: 4 -> 0; matrix products, arithmetic and copies ran while one was open for 3% -> 0% of each run, Pallas kernels for 0% -> 0%
where the time goes in v1:
time: 30.3 us; the launch traced here: 30.1 us
  Pallas kernels  27.7 us (91%)
  local copies, waits for them, and re-layouts  1.73 us (6%)
  between operations  0.7 us (2%)
    pallas_call x1, Pallas kernels, shards(): pl.pallas_call(functools.partial(tiles_kernel, sizes), out_shape=jax.Shap...  24.4 us
    pallas_call x1, Pallas kernels, shards(): pl.pallas_call(functools.partial(place_kernel, sizes, blocks), out_shape=...  3.29 us
    unnamed x10, local copies, waits for them, and re-layouts  1.73 us

profile of v1, /device:TPU:0, one launch (start us, length us, event | category | flops | bytes accessed | tf_op | source)
XLA Modules:
  0.0 30.1 jit_solution(1146400336093695685)
XLA Ops:
  0.7 0.0 copy-start.2
  0.7 0.0 copy-start.3
  0.7 0.0 copy-start.1
  0.7 0.7 %copy-done.2 = s32[2,4]{1,0:T(2,128)S(1)} copy-done((s32[2,4]{1,0:T(2,128)S(1)}, s32[2,4]{1,0:T(2,128)}, u32[]{:S(2)}) %copy-start.2) | copy-done | bytes 56
  1.3 0.0 copy-done.3
  1.3 0.0 copy-done.1
  1.4 0.0 copy-start
  1.4 1.0 %copy-done = s32[2,4,128,128]{3,2,1,0:T(8,128)S(1)} copy-done((s32[2,4,128,128]{3,2,1,0:T(8,128)S(1)}, s32[2,4,128,128]{3,2,1,0:T(8,128)}, u32[]{:S(2)}) %copy-start) | copy-done | bytes 524312
  2.4 0.0 copy-start.4
  2.4 24.4 %shard_map.64.tiles_ref = f32[2,4,2,32,128]{4,3,2,1,0:T(8,128)S(1)} custom-call(s32[2,4]{1,0:T(2,128)S(1)} %copy-done.1, s32[2,4]{1,0:T(2,128)S(1)} %copy-done.2, s32[2,4,128,128]{3,2,1,0:T(8,128)S(1)} %copy-done, s32[2,128]{1,0:T(2,128)S(1)} %bitcast.2), custom_call_target="tpu_custom_call" | custom-call | tf_op jit(solution)/shard_map/pallas_call | solution.py:315
  26.8 0.0 copy-done.4
  26.9 3.3 %shard_map.65 = f32[64,32,128]{2,1,0:T(8,128)} custom-call(s32[2,64]{1,0:T(2,128)S(1)} %bitcast.3, s32[1]{0:T(128)S(6)} %copy.7.count_ref, f32[2,4,2,32,128]{4,3,2,1,0:T(8,128)S(1)} %shard_map.64.tiles_ref), custom_call_target="tpu_custom_call" | custom-call | tf_op jit(solution)/shard_map/pallas_call | solution.py:348
Async XLA Ops:
  0.7 0.7 %copy-start.2 = (s32[2,4]{1,0:T(2,128)S(1)}, s32[2,4]{1,0:T(2,128)}, u32[]{:S(2)}) copy-start(s32[2,4]{1,0:T(2,128)} %ids_ref.1) | copy-start | bytes 100
  0.7 0.7 %copy-start.3 = (s32[256]{0:T(256)S(1)}, s32[256]{0:T(256)}, u32[]{:S(2)}) copy-start(s32[256]{0:T(256)} %param.9) | copy-start | bytes 3076
  0.7 0.7 %copy-start.1 = (s32[2,4]{1,0:T(2,128)S(1)}, s32[2,4]{1,0:T(2,128)}, u32[]{:S(2)}) copy-start(s32[2,4]{1,0:T(2,128)} %live_ref.1) | copy-start | bytes 100
  1.4 1.0 %copy-start = (s32[2,4,128,128]{3,2,1,0:T(8,128)S(1)}, s32[2,4,128,128]{3,2,1,0:T(8,128)}, u32[]{:S(2)}) copy-start(s32[2,4,128,128]{3,2,1,0:T(8,128)} %counts_ref.1) | copy-start | bytes 1572868
  2.4 24.4 %copy-start.4 = (s32[64,2]{0,1:T(2,128)S(1)}, s32[64,2]{0,1:T(2,128)}, u32[]{:S(2)}) copy-start(s32[64,2]{0,1:T(2,128)} %param.10) | copy-start | bytes 1540

commit v2 on v1

--- a/solution.py
+++ b/solution.py
@@ -7,6 +7,8 @@
 from jax.experimental.pallas import tpu as pltpu
 from jax.sharding import PartitionSpec as P
 
+steps = 32767.0
+tiny = 1e-30
 saturation = 1.2
 length_weight = 0.75
 epsilon = 1e-06
@@ -16,29 +18,39 @@
 
 def tiles_kernel(
     sizes,
+    live_hbm,
+    ids_hbm,
+    counts_hbm,
+    lengths_hbm,
+    out_ref,
     live_ref,
     ids_ref,
     counts_ref,
     lengths_ref,
-    out_ref,
     masked,
     small,
     right_counts,
     left_weight,
     right_weight,
     partial_sum,
+    coded,
+    scale_own,
     term_recv,
+    scale_recv,
     square_own,
     square_recv,
     column,
     final,
     pair_recv,
+    load_sem,
     small_send_sem,
     small_recv_sem,
     count_send_sem,
     count_recv_sem,
     term_send_sem,
     term_recv_sem,
+    scale_send_sem,
+    scale_recv_sem,
     square_send_sem,
     square_recv_sem,
     pair_send_sem,
@@ -85,10 +97,20 @@
 
     def term_copy(m, k):
         return pltpu.make_async_remote_copy(
-            src_ref=partial_sum.at[m, lax.rem(me_term + k, n_term)],
+            src_ref=coded.at[m, lax.rem(me_term + k, n_term)],
             dst_ref=term_recv.at[m, k],
             send_sem=term_send_sem.at[m, k],
             recv_sem=term_recv_sem.at[m, k],
+            device_id=term_peer(k),
+            device_id_type=MESH,
+        )
+
+    def scale_copy(k):
+        return pltpu.make_async_remote_copy(
+            src_ref=scale_own.at[lax.rem(me_term + k, n_term)],
+            dst_ref=scale_recv.at[k],
+            send_sem=scale_send_sem.at[k],
+            recv_sem=scale_recv_sem.at[k],
             device_id=term_peer(k),
             device_id_type=MESH,
         )
@@ -121,20 +143,35 @@
     for k in range(1, n_pair):
         pl.semaphore_signal(barrier, inc=1, device_id=pair_peer(k), device_id_type=MESH)
 
+    loads = [
+        pltpu.make_async_copy(live_hbm, live_ref, load_sem.at[0]),
+        pltpu.make_async_copy(ids_hbm, ids_ref, load_sem.at[1]),
+        pltpu.make_async_copy(lengths_hbm, lengths_ref, load_sem.at[2]),
+    ]
+    loads += [
+        pltpu.make_async_copy(counts_hbm.at[b], counts_ref.at[b], load_sem.at[3 + b])
+        for b in range(blocks)
+    ]
+    for load in loads:
+        load.start()
     small[0] = jnp.zeros(small.shape[1:], jnp.float32)
+    square_own[...] = jnp.zeros(square_own.shape, jnp.float32)
+    out_ref[out_ref.shape[0] - 1] = jnp.zeros(out_ref.shape[1:], jnp.float32)
+    for load in loads[:3]:
+        load.wait()
     for b in range(blocks):
+        loads[3 + b].wait()
         for s in range(slots):
-            live = jnp.full((rows, cols), live_ref[b, s], jnp.int32) > 0
+            live = jnp.broadcast_to(live_ref[b : b + 1, s : s + 1], (rows, cols)) > 0
             value = jnp.where(live, counts_ref[b, s].astype(jnp.float32), 0.0)
             masked[b, s] = value.astype(jnp.bfloat16)
             small[0, b, s : s + 1] = jnp.sum(
                 jnp.where(value > 0.0, 1.0, 0.0), axis=0, keepdims=True
             )
-            small[0, b, slots + s : slots + s + 1] = jnp.full(
-                (1, cols), ids_ref[b, s], jnp.int32
+            small[0, b, slots + s : slots + s + 1] = jnp.broadcast_to(
+                ids_ref[b : b + 1, s : s + 1], (1, cols)
             ).astype(jnp.float32)
     small[0, blocks, 0:blocks] = lengths_ref[...].astype(jnp.float32)
-    square_own[...] = jnp.zeros(square_own.shape, jnp.float32)
 
     pl.semaphore_wait(barrier, n_doc + n_term + n_pair - 3)
 
@@ -200,7 +237,12 @@
                     preferred_element_type=jnp.float32,
                 )
             for z in range(n_term):
-                partial_sum[m, z, b] = gram[z * part_rows : (z + 1) * part_rows]
+                piece = gram[z * part_rows : (z + 1) * part_rows]
+                top = jnp.maximum(jnp.max(piece, axis=0, keepdims=True), tiny)
+                partial_sum[m, z, b] = piece
+                code = (piece * (steps / top) + 0.5).astype(jnp.int32)
+                coded[m, z, b] = code.astype(jnp.int16)
+                scale_own[z, pl.ds(m * blocks + b, 1)] = top * (1.0 / steps)
         for k in range(1, n_term):
             term_copy(m, k).start()
 
@@ -226,19 +268,23 @@
 
     lax.fori_loop(1, n_doc, right_step, 0)
 
+    for k in range(1, n_term):
+        scale_copy(k).start()
     squares = square_own[...]
     for k in range(1, n_term):
         square_copy(k).wait_recv()
         squares = squares + square_recv[k]
     inverse = lax.rsqrt(squares + epsilon)
-    square_own_done = [square_copy(k) for k in range(1, n_term)]
-    for copy in square_own_done:
-        copy.wait_send()
+    for k in range(1, n_term):
+        square_copy(k).wait_send()
     square_own[...] = inverse
     left_scale = []
     for b in range(blocks):
         column[...] = jnp.transpose(jnp.broadcast_to(inverse[b : b + 1], (rows, rows)))
         left_scale.append(column[pl.ds(me_term * part_rows, part_rows)])
+
+    for k in range(1, n_term):
+        scale_copy(k).wait_recv()
 
     def finish(m, carry):
         for k in range(1, n_term):
@@ -247,10 +293,11 @@
         for b in range(blocks):
             total = partial_sum[m, me_term, b]
             for k in range(1, n_term):
-                total = total + term_recv[m, k, b]
+                scale = scale_recv[k, pl.ds(m * blocks + b, 1)]
+                total = total + term_recv[m, k, b].astype(jnp.float32) * scale
             value = total * left_scale[b] * right_scale
             final[m, b] = value
-            out_ref[0, m, b] = value
+            out_ref[m * blocks + b] = value
         for k in range(1, n_pair):
             pair_copy(m, k).start()
         return carry
@@ -260,7 +307,7 @@
     def collect(m, carry):
         for k in range(1, n_pair):
             pair_copy(m, k).wait_recv()
-            out_ref[k, m] = pair_recv[k, m]
+            out_ref[pl.ds((k * n_right + m) * blocks, blocks)] = pair_recv[k, m]
         for k in range(1, n_term):
             term_copy(m, k).wait_send()
         for k in range(1, n_pair):
@@ -268,37 +315,40 @@
         return carry
 
     lax.fori_loop(0, n_right, collect, 0)
+    for k in range(1, n_term):
+        scale_copy(k).wait_send()
     for k in range(1, n_doc):
         small_copy(k).wait_send()
         count_copy(k).wait_send()
 
 
-def place_kernel(sizes, blocks, pairs_ref, count_ref, tiles_ref, out_ref):
+def place_kernel(sizes, blocks, pairs_ref, count_ref, tiles_ref, out_ref, first_tile, sem):
     n_doc, n_term, n_pair = sizes
     per_core = blocks // n_pair
+    n_right = n_doc * per_core
     me_doc = lax.axis_index("doc")
     me_pair = lax.axis_index("pair")
     count = count_ref[0]
+    zero_tile = tiles_ref.shape[0] - 1
+
+    def fill(owner, carry):
+        k = lax.rem(me_doc - owner + n_doc, n_doc)
+        for inner in range(blocks):
+            side = lax.rem(me_pair - inner // per_core + n_pair, n_pair)
+            m = side * n_right + k * per_core + inner % per_core
+            first_tile[owner * blocks + inner] = (m - me_doc) * blocks
+        return carry
+
+    lax.fori_loop(0, n_doc, fill, 0)
 
     def step(row, carry):
-        live = row < count
-
-        @pl.when(live)
-        def _():
-            left = pairs_ref[0, row] - me_doc * blocks
-            right = pairs_ref[1, row]
-            owner, inner = right // blocks, right % blocks
-            side = lax.rem(me_pair - inner // per_core + n_pair, n_pair)
-            m = lax.rem(me_doc - owner + n_doc, n_doc) * per_core + inner % per_core
-            out_ref[row] = tiles_ref[side, m, left]
-
-        @pl.when(jnp.logical_not(live))
-        def _():
-            out_ref[row] = jnp.zeros(out_ref.shape[1:], jnp.float32)
-
+        tile = first_tile[pairs_ref[1, row]] + pairs_ref[0, row]
+        tile = jnp.where(row < count, tile, zero_tile)
+        pltpu.make_async_copy(tiles_ref.at[tile], out_ref.at[row], sem).start()
         return carry
 
-    lax.fori_loop(0, out_ref.shape[0], step, 0, unroll=4)
+    lax.fori_loop(0, out_ref.shape[0], step, 0, unroll=8)
+    pltpu.make_async_copy(out_ref, out_ref, sem).wait()
 
 
 def shards(sizes, counts, block_ids, live_slots, lengths, pairs, pair_count):
@@ -310,26 +360,36 @@
     table_rows = -(-max(2 * slots, blocks) // 8) * 8
     square_rows = -(-(blocks + n_right) // 8) * 8
     dma = pltpu.SemaphoreType.DMA
+    scale_rows = -(-(blocks * n_right) // 8) * 8
+    hbm = pl.BlockSpec(memory_space=pltpu.HBM)
     smem = pl.BlockSpec(memory_space=pltpu.SMEM)
     vmem = pl.BlockSpec(memory_space=pltpu.VMEM)
     tiles = pl.pallas_call(
         functools.partial(tiles_kernel, sizes),
-        out_shape=jax.ShapeDtypeStruct((n_pair, n_right, blocks, part_rows, rows), jnp.float32),
-        in_specs=[smem, smem, vmem, vmem],
+        out_shape=pltpu.VMEM((n_pair * n_right * blocks + 1, part_rows, rows), jnp.float32),
+        in_specs=[hbm, hbm, hbm, hbm],
         out_specs=vmem,
         scratch_shapes=[
+            pltpu.VMEM((blocks, slots), jnp.int32),
+            pltpu.VMEM((blocks, slots), jnp.int32),
+            pltpu.VMEM((blocks, slots, rows, cols), jnp.int32),
+            pltpu.VMEM((blocks, rows), jnp.int32),
             pltpu.VMEM((blocks, slots, rows, cols), jnp.bfloat16),
             pltpu.VMEM((n_doc, blocks + 1, table_rows, cols), jnp.float32),
             pltpu.VMEM((n_doc, per_core, slots, rows, cols), jnp.bfloat16),
             pltpu.VMEM((blocks, slots, rows, cols), jnp.bfloat16),
             pltpu.VMEM((slots, rows, cols), jnp.bfloat16),
             pltpu.VMEM((n_right, n_term, blocks, part_rows, rows), jnp.float32),
-            pltpu.VMEM((n_right, n_term, blocks, part_rows, rows), jnp.float32),
+            pltpu.VMEM((n_right, n_term, blocks, part_rows, rows), jnp.int16),
+            pltpu.VMEM((n_term, scale_rows, rows), jnp.float32),
+            pltpu.VMEM((n_right, n_term, blocks, part_rows, rows), jnp.int16),
+            pltpu.VMEM((n_term, scale_rows, rows), jnp.float32),
             pltpu.VMEM((square_rows, rows), jnp.float32),
             pltpu.VMEM((n_term, square_rows, rows), jnp.float32),
             pltpu.VMEM((rows, rows), jnp.float32),
             pltpu.VMEM((n_right, blocks, part_rows, rows), jnp.float32),
             pltpu.VMEM((n_pair, n_right, blocks, part_rows, rows), jnp.float32),
+            dma((3 + blocks,)),
             dma((n_doc,)),
             dma((n_doc,)),
             dma((n_doc,)),
@@ -338,18 +398,21 @@
             dma((n_right, n_term)),
             dma((n_term,)),
             dma((n_term,)),
+            dma((n_term,)),
+            dma((n_term,)),
             dma((n_right, n_pair)),
             dma((n_right, n_pair)),
         ],
         compiler_params=pltpu.CompilerParams(
             collective_id=0, has_side_effects=True, vmem_limit_bytes=48 * 1024 * 1024
         ),
-    )(live_slots, block_ids, counts, lengths.reshape(blocks, rows))
+    )(*[pltpu.with_memory_space_constraint(x, pltpu.HBM) for x in (live_slots, block_ids, counts, lengths.reshape(blocks, rows))])
     return pl.pallas_call(
         functools.partial(place_kernel, sizes, blocks),
         out_shape=jax.ShapeDtypeStruct((pairs.shape[0], part_rows, rows), jnp.float32),
-        in_specs=[smem, smem, vmem],
-        out_specs=vmem,
+        in_specs=[smem, smem, pl.BlockSpec(memory_space=pl.ANY)],
+        out_specs=hbm,
+        scratch_shapes=[pltpu.SMEM((n_doc * blocks,), jnp.int32), dma(())],
         compiler_params=pltpu.CompilerParams(vmem_limit_bytes=48 * 1024 * 1024),
     )(pairs.T, pair_count, tiles)
 

time: 30.3 us -> 22.9 us (0.76)
  Pallas kernels: 27.7 us -> 22.1 us
  local copies, waits for them, and re-layouts: 1.73 us -> 0.01 us
    pallas_call x1, Pallas kernels: 24.4 us -> 20.5 us  [shards(): pl.pallas_call(functools.partial(tiles_kernel, sizes), out_shape=pltpu.VM...]
    pallas_call x1, Pallas kernels: 3.29 us -> 1.56 us  [shards(): pl.pallas_call(functools.partial(place_kernel, sizes, blocks), out_shape=...]
    unnamed x10 -> x2, local copies, waits for them, and re-layouts: 1.73 us -> 0.01 us
where the time goes in v2:
time: 22.9 us; the launch traced here: 22.7 us
  Pallas kernels  22.1 us (97%)
  between operations  0.68 us (3%)
    pallas_call x1, Pallas kernels, shards(): pl.pallas_call(functools.partial(tiles_kernel, sizes), out_shape=pltpu.VM...  20.5 us
    pallas_call x1, Pallas kernels, shards(): pl.pallas_call(functools.partial(place_kernel, sizes, blocks), out_shape=...  1.56 us

profile of v2, /device:TPU:0, one launch (start us, length us, event | category | flops | bytes accessed | tf_op | source)
XLA Modules:
  0.0 22.7 jit_solution(12926222753423742459)
XLA Ops:
  0.7 0.0 copy-start
  0.7 20.5 %shard_map.64.tiles_ref = f32[17,32,128]{2,1,0:T(8,128)S(1)} custom-call(s32[2,4]{1,0:T(2,128)} %live_hbm.1, s32[2,4]{1,0:T(2,128)} %ids_hbm.1, s32[2,4,128,128]{3,2,1,0:T(8,128)} %counts_hbm.1, s32[2,128]{1,0:T(2,128)} %bitcast.3), custom_call_target="tpu_custom_call" | custom-call | tf_op jit(solution)/shard_map/pallas_call | solution.py:367
  21.2 0.0 copy-done
  21.2 1.6 %shard_map.65 = f32[64,32,128]{2,1,0:T(8,128)} custom-call(s32[2,64]{1,0:T(2,128)S(1)} %bitcast.2, s32[1]{0:T(128)S(6)} %copy.7.count_ref, f32[17,32,128]{2,1,0:T(8,128)S(1)} %shard_map.64.tiles_ref), custom_call_target="tpu_custom_call" | custom-call | tf_op jit(solution)/shard_map/pallas_call | solution.py:410
Async XLA Ops:
  0.7 20.5 %copy-start = (s32[64,2]{0,1:T(2,128)S(1)}, s32[64,2]{0,1:T(2,128)}, u32[]{:S(2)}) copy-start(s32[64,2]{0,1:T(2,128)} %param.10) | copy-start | bytes 1540

commit v3 on v2

--- a/solution.py
+++ b/solution.py
@@ -14,6 +14,27 @@
 epsilon = 1e-06
 
 MESH = pl.DeviceIdType.MESH
+
+
+def exclusive_or(a, b, count):
+    result, bit = 0, 1
+    while bit < count:
+        x, y = lax.rem(a // bit, 2), lax.rem(b // bit, 2)
+        result = result + bit * (x + y - 2 * x * y)
+        bit *= 2
+    return result
+
+
+def target_of(me, k, count):
+    if count & (count - 1):
+        return lax.rem(me + k, count)
+    return exclusive_or(me, k, count)
+
+
+def slot_of(me, owner, count):
+    if count & (count - 1):
+        return lax.rem(me - owner + count, count)
+    return exclusive_or(me, owner, count)
 
 
 def tiles_kernel(
@@ -32,13 +53,16 @@
     right_counts,
     left_weight,
     right_weight,
+    aligned,
+    freq_table,
+    length_table,
     partial_sum,
     coded,
-    scale_own,
     term_recv,
-    scale_recv,
+    side_own,
+    side_recv,
     square_own,
-    square_recv,
+    inverse_ref,
     column,
     final,
     pair_recv,
@@ -49,10 +73,8 @@
     count_recv_sem,
     term_send_sem,
     term_recv_sem,
-    scale_send_sem,
-    scale_recv_sem,
-    square_send_sem,
-    square_recv_sem,
+    side_send_sem,
+    side_recv_sem,
     pair_send_sem,
     pair_recv_sem,
 ):
@@ -67,7 +89,7 @@
     me_pair = lax.axis_index("pair")
 
     def doc_peer(k):
-        return {"doc": lax.rem(me_doc + k, n_doc)}
+        return {"doc": target_of(me_doc, k, n_doc)}
 
     def term_peer(k):
         return {"term": lax.rem(me_term + k, n_term)}
@@ -105,22 +127,12 @@
             device_id_type=MESH,
         )
 
-    def scale_copy(k):
+    def side_copy(k):
         return pltpu.make_async_remote_copy(
-            src_ref=scale_own.at[lax.rem(me_term + k, n_term)],
-            dst_ref=scale_recv.at[k],
-            send_sem=scale_send_sem.at[k],
-            recv_sem=scale_recv_sem.at[k],
-            device_id=term_peer(k),
-            device_id_type=MESH,
-        )
-
-    def square_copy(k):
-        return pltpu.make_async_remote_copy(
-            src_ref=square_own,
-            dst_ref=square_recv.at[k],
-            send_sem=square_send_sem.at[k],
-            recv_sem=square_recv_sem.at[k],
+            src_ref=side_own.at[lax.rem(me_term + k, n_term)],
+            dst_ref=side_recv.at[k],
+            send_sem=side_send_sem.at[k],
+            recv_sem=side_recv_sem.at[k],
             device_id=term_peer(k),
             device_id_type=MESH,
         )
@@ -177,7 +189,8 @@
 
     for k in range(1, n_doc):
         small_copy(k).start()
-    for k in range(1, n_doc):
+    first = [k for k in range(1, n_doc) if k & (k - 1) == 0]
+    for k in first:
         count_copy(k).start()
     for k in range(1, n_doc):
         small_copy(k).wait_recv()
@@ -199,101 +212,115 @@
                     acc = acc + jnp.where(same, table[s : s + 1], 0.0)
             return acc
 
-        freq = lax.fori_loop(0, n_doc, add, jnp.zeros(ids.shape, jnp.float32))
+        freq = lax.fori_loop(
+            0, n_doc, add, jnp.zeros(ids.shape, jnp.float32), unroll=min(n_doc, 4)
+        )
         return jnp.log(1.0 + (docs_all - freq + 0.5) / (freq + 0.5))
 
-    def weigh(k, b, read, target, square_row):
-        inv_freq = inv_freq_of(small[k, b, slots : 2 * slots]) * (saturation + 1.0)
+    def prepare(k, b, place):
+        freq_table[place] = inv_freq_of(small[k, b, slots : 2 * slots]) * (saturation + 1.0)
         length = small[k, blocks, pl.ds(b, 1)]
         scale = saturation * (1.0 - length_weight + length_weight * length / avg_len)
-        scale = jnp.transpose(jnp.broadcast_to(scale, (rows, rows)))
+        length_table[place] = jnp.transpose(jnp.broadcast_to(scale, (rows, rows)))
+
+    def weigh(read, target, place):
         squares = jnp.zeros((rows, cols), jnp.float32)
         for s in range(slots):
             freq = read(s).astype(jnp.float32)
-            weight = inv_freq[s : s + 1] * freq / (freq + scale)
+            weight = freq_table[place, s : s + 1] * freq / (freq + length_table[place])
             squares = squares + weight * weight
             target[s] = weight.astype(jnp.bfloat16)
-        square_own[pl.ds(square_row, 1)] = jnp.sum(
-            jnp.transpose(squares), axis=0, keepdims=True
-        )
-
-    for b in range(blocks):
-        weigh(0, b, lambda s, b=b: masked[b, s], left_weight.at[b], b)
+        return squares
+
+    def keep_squares(squares, place):
+        square_own[pl.ds(place, 1)] = jnp.sum(jnp.transpose(squares), axis=0, keepdims=True)
 
     def grams(m, right, right_ids):
         for b in range(blocks):
             left_ids = small[0, b, slots : 2 * slots]
-            gram = jnp.zeros((rows, rows), jnp.float32)
-            for i in range(slots):
-                aligned = jnp.zeros((rows, cols), jnp.bfloat16)
-                for j in range(slots):
+            for j in range(slots):
+                total = jnp.zeros((rows, cols), jnp.bfloat16)
+                for i in range(slots):
                     same = left_ids[i : i + 1] == right_ids[j : j + 1]
                     same = jnp.where(same, 1.0, 0.0).astype(jnp.bfloat16)
-                    aligned = aligned + right[j] * same
-                gram = gram + lax.dot_general(
-                    left_weight[b, i],
-                    aligned,
-                    (((1,), (1,)), ((), ())),
-                    preferred_element_type=jnp.float32,
-                )
-            for z in range(n_term):
-                piece = gram[z * part_rows : (z + 1) * part_rows]
+                    total = total + left_weight[b, i] * same
+                aligned[b * rows : (b + 1) * rows, j * cols : (j + 1) * cols] = total
+        gram = lax.dot_general(
+            aligned[...],
+            jnp.concatenate([right[j] for j in range(slots)], axis=1),
+            (((1,), (1,)), ((), ())),
+            preferred_element_type=jnp.float32,
+        )
+        for z in range(n_term):
+            for b in range(blocks):
+                start = b * rows + z * part_rows
+                piece = gram[start : start + part_rows]
                 top = jnp.maximum(jnp.max(piece, axis=0, keepdims=True), tiny)
                 partial_sum[m, z, b] = piece
                 code = (piece * (steps / top) + 0.5).astype(jnp.int32)
                 coded[m, z, b] = code.astype(jnp.int16)
-                scale_own[z, pl.ds(m * blocks + b, 1)] = top * (1.0 / steps)
+                side_own[z, pl.ds(m * blocks + b, 1)] = top * (1.0 / steps)
         for k in range(1, n_term):
             term_copy(m, k).start()
 
+    for b in range(blocks):
+        prepare(0, b, b)
+    left_squares = [
+        weigh(lambda s, b=b: masked[b, s], left_weight.at[b], b) for b in range(blocks)
+    ]
     for i in range(per_core):
         own = me_pair * per_core + i
-        square_own[pl.ds(blocks + i, 1)] = square_own[pl.ds(own, 1)]
         grams(i, left_weight.at[own], small[0, own, slots : 2 * slots])
+    for k in range(1, n_doc):
+        if k not in first:
+            count_copy(k).start()
+    for b in range(blocks):
+        keep_squares(left_squares[b], b)
+    for i in range(per_core):
+        square_own[pl.ds(blocks + i, 1)] = square_own[pl.ds(me_pair * per_core + i, 1)]
+
+    def prepare_right(k, carry):
+        for i in range(per_core):
+            prepare(k, me_pair * per_core + i, blocks + k * per_core + i)
+        return carry
+
+    lax.fori_loop(1, n_doc, prepare_right, 0)
 
     def right_step(k, carry):
         count_copy(k).wait_recv()
         for i in range(per_core):
-            b = me_pair * per_core + i
             m = k * per_core + i
-            weigh(k, b, lambda s, i=i: right_counts[k, i, s], right_weight, blocks + m)
-
-            @pl.when(m == n_right - 1)
-            def _():
-                for t in range(1, n_term):
-                    square_copy(t).start()
-
-            grams(m, right_weight, small[k, b, slots : 2 * slots])
+            squares = weigh(lambda s, i=i: right_counts[k, i, s], right_weight, blocks + m)
+            grams(m, right_weight, small[k, me_pair * per_core + i, slots : 2 * slots])
+            keep_squares(squares, blocks + m)
         return carry
 
     lax.fori_loop(1, n_doc, right_step, 0)
 
+    scale_rows = side_own.shape[1] - square_own.shape[0]
+    squares = square_own[...]
+    for z in range(n_term):
+        side_own[z, scale_rows:] = squares
     for k in range(1, n_term):
-        scale_copy(k).start()
-    squares = square_own[...]
+        side_copy(k).start()
     for k in range(1, n_term):
-        square_copy(k).wait_recv()
-        squares = squares + square_recv[k]
+        side_copy(k).wait_recv()
+        squares = squares + side_recv[k, scale_rows:]
     inverse = lax.rsqrt(squares + epsilon)
-    for k in range(1, n_term):
-        square_copy(k).wait_send()
-    square_own[...] = inverse
+    inverse_ref[...] = inverse
     left_scale = []
     for b in range(blocks):
         column[...] = jnp.transpose(jnp.broadcast_to(inverse[b : b + 1], (rows, rows)))
         left_scale.append(column[pl.ds(me_term * part_rows, part_rows)])
 
-    for k in range(1, n_term):
-        scale_copy(k).wait_recv()
-
     def finish(m, carry):
         for k in range(1, n_term):
             term_copy(m, k).wait_recv()
-        right_scale = square_own[pl.ds(blocks + m, 1)]
+        right_scale = inverse_ref[pl.ds(blocks + m, 1)]
         for b in range(blocks):
             total = partial_sum[m, me_term, b]
             for k in range(1, n_term):
-                scale = scale_recv[k, pl.ds(m * blocks + b, 1)]
+                scale = side_recv[k, pl.ds(m * blocks + b, 1)]
                 total = total + term_recv[m, k, b].astype(jnp.float32) * scale
             value = total * left_scale[b] * right_scale
             final[m, b] = value
@@ -316,7 +343,7 @@
 
     lax.fori_loop(0, n_right, collect, 0)
     for k in range(1, n_term):
-        scale_copy(k).wait_send()
+        side_copy(k).wait_send()
     for k in range(1, n_doc):
         small_copy(k).wait_send()
         count_copy(k).wait_send()
@@ -332,7 +359,7 @@
     zero_tile = tiles_ref.shape[0] - 1
 
     def fill(owner, carry):
-        k = lax.rem(me_doc - owner + n_doc, n_doc)
+        k = slot_of(me_doc, owner, n_doc)
         for inner in range(blocks):
             side = lax.rem(me_pair - inner // per_core + n_pair, n_pair)
             m = side * n_right + k * per_core + inner % per_core
@@ -379,13 +406,16 @@
             pltpu.VMEM((n_doc, per_core, slots, rows, cols), jnp.bfloat16),
             pltpu.VMEM((blocks, slots, rows, cols), jnp.bfloat16),
             pltpu.VMEM((slots, rows, cols), jnp.bfloat16),
+            pltpu.VMEM((blocks * rows, slots * cols), jnp.bfloat16),
+            pltpu.VMEM((blocks + n_right, slots, cols), jnp.float32),
+            pltpu.VMEM((blocks + n_right, rows, rows), jnp.float32),
             pltpu.VMEM((n_right, n_term, blocks, part_rows, rows), jnp.float32),
             pltpu.VMEM((n_right, n_term, blocks, part_rows, rows), jnp.int16),
-            pltpu.VMEM((n_term, scale_rows, rows), jnp.float32),
             pltpu.VMEM((n_right, n_term, blocks, part_rows, rows), jnp.int16),
-            pltpu.VMEM((n_term, scale_rows, rows), jnp.float32),
+            pltpu.VMEM((n_term, scale_rows + square_rows, rows), jnp.float32),
+            pltpu.VMEM((n_term, scale_rows + square_rows, rows), jnp.float32),
             pltpu.VMEM((square_rows, rows), jnp.float32),
-            pltpu.VMEM((n_term, square_rows, rows), jnp.float32),
+            pltpu.VMEM((square_rows, rows), jnp.float32),
             pltpu.VMEM((rows, rows), jnp.float32),
             pltpu.VMEM((n_right, blocks, part_rows, rows), jnp.float32),
             pltpu.VMEM((n_pair, n_right, blocks, part_rows, rows), jnp.float32),
@@ -396,8 +426,6 @@
             dma((n_doc,)),
             dma((n_right, n_term)),
             dma((n_right, n_term)),
-            dma((n_term,)),
-            dma((n_term,)),
             dma((n_term,)),
             dma((n_term,)),
             dma((n_right, n_pair)),

time: 22.9 us -> 23 us (level)
  no operation moved by 1% of the time
where the time goes in v3:
time: 23 us; the launch traced here: 22.9 us
  Pallas kernels  22.2 us (97%)
  between operations  0.68 us (3%)
    pallas_call x1, Pallas kernels, shards(): pl.pallas_call(functools.partial(tiles_kernel, sizes), out_shape=pltpu.VM...  20.6 us
    pallas_call x1, Pallas kernels, shards(): pl.pallas_call(functools.partial(place_kernel, sizes, blocks), out_shape=...  1.61 us

profile of v3, /device:TPU:0, one launch (start us, length us, event | category | flops | bytes accessed | tf_op | source)
XLA Modules:
  0.0 22.9 jit_solution(2304745345602515506)
XLA Ops:
  0.7 0.0 copy-start
  0.7 20.6 %shard_map.64.tiles_ref = f32[17,32,128]{2,1,0:T(8,128)S(1)} custom-call(s32[2,4]{1,0:T(2,128)} %live_hbm.1, s32[2,4]{1,0:T(2,128)} %ids_hbm.1, s32[2,4,128,128]{3,2,1,0:T(8,128)} %counts_hbm.1, s32[2,128]{1,0:T(2,128)} %bitcast.3), custom_call_target="tpu_custom_call" | custom-call | tf_op jit(solution)/shard_map/pallas_call | solution.py:394
  21.3 0.0 copy-done
  21.3 1.6 %shard_map.65 = f32[64,32,128]{2,1,0:T(8,128)} custom-call(s32[2,64]{1,0:T(2,128)S(1)} %bitcast.2, s32[1]{0:T(128)S(6)} %copy.7.count_ref, f32[17,32,128]{2,1,0:T(8,128)S(1)} %shard_map.64.tiles_ref), custom_call_target="tpu_custom_call" | custom-call | tf_op jit(solution)/shard_map/pallas_call | solution.py:438
Async XLA Ops:
  0.7 20.6 %copy-start = (s32[64,2]{0,1:T(2,128)S(1)}, s32[64,2]{0,1:T(2,128)}, u32[]{:S(2)}) copy-start(s32[64,2]{0,1:T(2,128)} %param.10) | copy-start | bytes 1540

commit v4 on v3

--- a/solution.py
+++ b/solution.py
@@ -54,6 +54,7 @@
     left_weight,
     right_weight,
     aligned,
+    ids_table,
     freq_table,
     length_table,
     partial_sum,
@@ -63,7 +64,6 @@
     side_recv,
     square_own,
     inverse_ref,
-    column,
     final,
     pair_recv,
     load_sem,
@@ -189,12 +189,15 @@
 
     for k in range(1, n_doc):
         small_copy(k).start()
-    first = [k for k in range(1, n_doc) if k & (k - 1) == 0]
-    for k in first:
+    for k in sorted(range(1, n_doc), key=lambda k: k & (k - 1) != 0):
         count_copy(k).start()
     for k in range(1, n_doc):
         small_copy(k).wait_recv()
 
+    row_at = lax.broadcasted_iota(jnp.int32, (rows, cols), 0)
+    col_at = lax.broadcasted_iota(jnp.int32, (rows, cols), 1)
+    diagonal = row_at == col_at
+    part_diagonal = row_at[:part_rows] + me_term * part_rows == col_at[:part_rows]
     total_len = lax.fori_loop(
         0,
         n_doc,
@@ -203,37 +206,52 @@
     )
     avg_len = jnp.sum(total_len, axis=1, keepdims=True) / docs_all
 
-    def inv_freq_of(ids):
-        def add(k, acc):
-            for b in range(blocks):
-                table = small[k, b]
-                for s in range(slots):
-                    same = ids == table[slots + s : slots + s + 1]
-                    acc = acc + jnp.where(same, table[s : s + 1], 0.0)
-            return acc
-
-        freq = lax.fori_loop(
-            0, n_doc, add, jnp.zeros(ids.shape, jnp.float32), unroll=min(n_doc, 4)
-        )
-        return jnp.log(1.0 + (docs_all - freq + 0.5) / (freq + 0.5))
-
-    def prepare(k, b, place):
-        freq_table[place] = inv_freq_of(small[k, b, slots : 2 * slots]) * (saturation + 1.0)
+    def table_row(k, b, place):
+        ids_table[pl.ds(place * slots, slots)] = small[k, b, slots : 2 * slots]
         length = small[k, blocks, pl.ds(b, 1)]
         scale = saturation * (1.0 - length_weight + length_weight * length / avg_len)
-        length_table[place] = jnp.transpose(jnp.broadcast_to(scale, (rows, rows)))
+        scale = jnp.sum(jnp.where(diagonal, scale, 0.0), axis=1, keepdims=True)
+        length_table[place] = jnp.broadcast_to(scale, (rows, cols))
+
+    for b in range(blocks):
+        table_row(0, b, b)
+
+    def right_rows(k, carry):
+        for i in range(per_core):
+            table_row(k, me_pair * per_core + i, blocks + k * per_core + i)
+        return carry
+
+    lax.fori_loop(0, n_doc, right_rows, 0, unroll=min(n_doc, 4))
+    ids = ids_table[...]
+
+    def add(k, acc):
+        for b in range(blocks):
+            table = small[k, b]
+            for s in range(slots):
+                same = ids == table[slots + s : slots + s + 1]
+                acc = acc + jnp.where(same, table[s : s + 1], 0.0)
+        return acc
+
+    doc_freq = lax.fori_loop(
+        0, n_doc, add, jnp.zeros(ids.shape, jnp.float32), unroll=min(n_doc, 4)
+    )
+    freq_table[...] = jnp.log(1.0 + (docs_all - doc_freq + 0.5) / (doc_freq + 0.5)) * (
+        saturation + 1.0
+    )
 
     def weigh(read, target, place):
         squares = jnp.zeros((rows, cols), jnp.float32)
         for s in range(slots):
             freq = read(s).astype(jnp.float32)
-            weight = freq_table[place, s : s + 1] * freq / (freq + length_table[place])
+            weight = freq_table[pl.ds(place * slots + s, 1)] * freq / (freq + length_table[place])
             squares = squares + weight * weight
             target[s] = weight.astype(jnp.bfloat16)
         return squares
 
     def keep_squares(squares, place):
-        square_own[pl.ds(place, 1)] = jnp.sum(jnp.transpose(squares), axis=0, keepdims=True)
+        squares = jnp.sum(squares, axis=1, keepdims=True)
+        squares = jnp.where(diagonal, squares, 0.0)
+        square_own[pl.ds(place, 1)] = jnp.sum(squares, axis=0, keepdims=True)
 
     def grams(m, right, right_ids):
         for b in range(blocks):
@@ -263,28 +281,16 @@
         for k in range(1, n_term):
             term_copy(m, k).start()
 
-    for b in range(blocks):
-        prepare(0, b, b)
     left_squares = [
         weigh(lambda s, b=b: masked[b, s], left_weight.at[b], b) for b in range(blocks)
     ]
     for i in range(per_core):
         own = me_pair * per_core + i
         grams(i, left_weight.at[own], small[0, own, slots : 2 * slots])
-    for k in range(1, n_doc):
-        if k not in first:
-            count_copy(k).start()
     for b in range(blocks):
         keep_squares(left_squares[b], b)
     for i in range(per_core):
         square_own[pl.ds(blocks + i, 1)] = square_own[pl.ds(me_pair * per_core + i, 1)]
-
-    def prepare_right(k, carry):
-        for i in range(per_core):
-            prepare(k, me_pair * per_core + i, blocks + k * per_core + i)
-        return carry
-
-    lax.fori_loop(1, n_doc, prepare_right, 0)
 
     def right_step(k, carry):
         count_copy(k).wait_recv()
@@ -310,8 +316,8 @@
     inverse_ref[...] = inverse
     left_scale = []
     for b in range(blocks):
-        column[...] = jnp.transpose(jnp.broadcast_to(inverse[b : b + 1], (rows, rows)))
-        left_scale.append(column[pl.ds(me_term * part_rows, part_rows)])
+        picked = jnp.where(part_diagonal, inverse[b : b + 1], 0.0)
+        left_scale.append(jnp.sum(picked, axis=1, keepdims=True))
 
     def finish(m, carry):
         for k in range(1, n_term):
@@ -407,7 +413,8 @@
             pltpu.VMEM((blocks, slots, rows, cols), jnp.bfloat16),
             pltpu.VMEM((slots, rows, cols), jnp.bfloat16),
             pltpu.VMEM((blocks * rows, slots * cols), jnp.bfloat16),
-            pltpu.VMEM((blocks + n_right, slots, cols), jnp.float32),
+            pltpu.VMEM(((blocks + n_right) * slots, cols), jnp.float32),
+            pltpu.VMEM(((blocks + n_right) * slots, cols), jnp.float32),
             pltpu.VMEM((blocks + n_right, rows, rows), jnp.float32),
             pltpu.VMEM((n_right, n_term, blocks, part_rows, rows), jnp.float32),
             pltpu.VMEM((n_right, n_term, blocks, part_rows, rows), jnp.int16),
@@ -416,7 +423,6 @@
             pltpu.VMEM((n_term, scale_rows + square_rows, rows), jnp.float32),
             pltpu.VMEM((square_rows, rows), jnp.float32),
             pltpu.VMEM((square_rows, rows), jnp.float32),
-            pltpu.VMEM((rows, rows), jnp.float32),
             pltpu.VMEM((n_right, blocks, part_rows, rows), jnp.float32),
             pltpu.VMEM((n_pair, n_right, blocks, part_rows, rows), jnp.float32),
             dma((3 + blocks,)),

time: 23 us -> 22.6 us (0.983)
  Pallas kernels: 22.2 us -> 21.7 us
    pallas_call x1, Pallas kernels: 20.6 us -> 20.1 us  [shards(): pl.pallas_call(functools.partial(tiles_kernel, sizes), out_shape=pltpu.VM...]
where the time goes in v4:
time: 22.6 us; the launch traced here: 22.4 us
  Pallas kernels  21.7 us (96%)
  between operations  0.68 us (3%)
    pallas_call x1, Pallas kernels, shards(): pl.pallas_call(functools.partial(tiles_kernel, sizes), out_shape=pltpu.VM...  20.1 us
    pallas_call x1, Pallas kernels, shards(): pl.pallas_call(functools.partial(place_kernel, sizes, blocks), out_shape=...  1.61 us

profile of v4, /device:TPU:0, one launch (start us, length us, event | category | flops | bytes accessed | tf_op | source)
XLA Modules:
  0.0 22.4 jit_solution(3328876851679214417)
XLA Ops:
  0.7 0.0 copy-start
  0.7 20.1 %shard_map.64.tiles_ref = f32[17,32,128]{2,1,0:T(8,128)S(1)} custom-call(s32[2,4]{1,0:T(2,128)} %live_hbm.1, s32[2,4]{1,0:T(2,128)} %ids_hbm.1, s32[2,4,128,128]{3,2,1,0:T(8,128)} %counts_hbm.1, s32[2,128]{1,0:T(2,128)} %bitcast.3), custom_call_target="tpu_custom_call" | custom-call | tf_op jit(solution)/shard_map/pallas_call | solution.py:400
  20.8 0.0 copy-done
  20.8 1.6 %shard_map.65 = f32[64,32,128]{2,1,0:T(8,128)} custom-call(s32[2,64]{1,0:T(2,128)S(1)} %bitcast.2, s32[1]{0:T(128)S(6)} %copy.7.count_ref, f32[17,32,128]{2,1,0:T(8,128)S(1)} %shard_map.64.tiles_ref), custom_call_target="tpu_custom_call" | custom-call | tf_op jit(solution)/shard_map/pallas_call | solution.py:444
Async XLA Ops:
  0.7 20.1 %copy-start = (s32[64,2]{0,1:T(2,128)S(1)}, s32[64,2]{0,1:T(2,128)}, u32[]{:S(2)}) copy-start(s32[64,2]{0,1:T(2,128)} %param.10) | copy-start | bytes 1540

commit v5 on v4

--- a/solution.py
+++ b/solution.py
@@ -43,11 +43,16 @@
     ids_hbm,
     counts_hbm,
     lengths_hbm,
+    pairs_hbm,
+    limit_ref,
     out_ref,
+    tile_ref,
     live_ref,
     ids_ref,
     counts_ref,
     lengths_ref,
+    pairs_ref,
+    number_ref,
     masked,
     small,
     right_counts,
@@ -117,6 +122,20 @@
             device_id_type=MESH,
         )
 
+    relay = n_doc == 4
+    near = 1 + lax.rem(me_pair, 2)
+    far = 3 - near
+
+    def relay_copy():
+        return pltpu.make_async_remote_copy(
+            src_ref=right_counts.at[near],
+            dst_ref=right_counts.at[3],
+            send_sem=count_send_sem.at[3],
+            recv_sem=count_recv_sem.at[3],
+            device_id=doc_peer(far),
+            device_id_type=MESH,
+        )
+
     def term_copy(m, k):
         return pltpu.make_async_remote_copy(
             src_ref=coded.at[m, lax.rem(me_term + k, n_term)],
@@ -160,11 +179,12 @@
         pltpu.make_async_copy(ids_hbm, ids_ref, load_sem.at[1]),
         pltpu.make_async_copy(lengths_hbm, lengths_ref, load_sem.at[2]),
     ]
+    extra = [pltpu.make_async_copy(pairs_hbm, pairs_ref, load_sem.at[3 + blocks])]
     loads += [
         pltpu.make_async_copy(counts_hbm.at[b], counts_ref.at[b], load_sem.at[3 + b])
         for b in range(blocks)
     ]
-    for load in loads:
+    for load in loads + extra:
         load.start()
     small[0] = jnp.zeros(small.shape[1:], jnp.float32)
     square_own[...] = jnp.zeros(square_own.shape, jnp.float32)
@@ -189,7 +209,7 @@
 
     for k in range(1, n_doc):
         small_copy(k).start()
-    for k in sorted(range(1, n_doc), key=lambda k: k & (k - 1) != 0):
+    for k in (near, far) if relay else range(1, n_doc):
         count_copy(k).start()
     for k in range(1, n_doc):
         small_copy(k).wait_recv()
@@ -284,6 +304,24 @@
     left_squares = [
         weigh(lambda s, b=b: masked[b, s], left_weight.at[b], b) for b in range(blocks)
     ]
+    for load in extra:
+        load.wait()
+    left = pairs_ref[0:1]
+    right = pairs_ref[1:2]
+    number = left - me_doc * blocks
+    for block in range(n_doc * blocks):
+        owner, inner = block // blocks, block % blocks
+        side = lax.rem(me_pair - inner // per_core + n_pair, n_pair)
+        m = slot_of(me_doc, owner, n_doc) * per_core + inner % per_core
+        number = number + jnp.where(right == block, (side * n_right + m) * blocks, 0)
+    row = lax.broadcasted_iota(jnp.int32, number.shape, 1)
+    number_ref[...] = jnp.where(row < limit_ref[0], number, out_ref.shape[0] - 1)
+    number_copy = pltpu.make_async_copy(number_ref, tile_ref, load_sem.at[4 + blocks])
+    number_copy.start()
+
+    if relay:
+        count_copy(near).wait_recv()
+        relay_copy().start()
     for i in range(per_core):
         own = me_pair * per_core + i
         grams(i, left_weight.at[own], small[0, own, slots : 2 * slots])
@@ -292,8 +330,20 @@
     for i in range(per_core):
         square_own[pl.ds(blocks + i, 1)] = square_own[pl.ds(me_pair * per_core + i, 1)]
 
-    def right_step(k, carry):
-        count_copy(k).wait_recv()
+    def right_step(step, carry):
+        if relay:
+            k = jnp.where(step == 1, near, jnp.where(step == 2, far, 3))
+
+            @pl.when(step == 2)
+            def _():
+                count_copy(far).wait_recv()
+
+            @pl.when(step == 3)
+            def _():
+                relay_copy().wait_recv()
+        else:
+            k = step
+            count_copy(k).wait_recv()
         for i in range(per_core):
             m = k * per_core + i
             squares = weigh(lambda s, i=i: right_counts[k, i, s], right_weight, blocks + m)
@@ -348,35 +398,20 @@
         return carry
 
     lax.fori_loop(0, n_right, collect, 0)
+    number_copy.wait()
     for k in range(1, n_term):
         side_copy(k).wait_send()
     for k in range(1, n_doc):
         small_copy(k).wait_send()
-        count_copy(k).wait_send()
-
-
-def place_kernel(sizes, blocks, pairs_ref, count_ref, tiles_ref, out_ref, first_tile, sem):
-    n_doc, n_term, n_pair = sizes
-    per_core = blocks // n_pair
-    n_right = n_doc * per_core
-    me_doc = lax.axis_index("doc")
-    me_pair = lax.axis_index("pair")
-    count = count_ref[0]
-    zero_tile = tiles_ref.shape[0] - 1
-
-    def fill(owner, carry):
-        k = slot_of(me_doc, owner, n_doc)
-        for inner in range(blocks):
-            side = lax.rem(me_pair - inner // per_core + n_pair, n_pair)
-            m = side * n_right + k * per_core + inner % per_core
-            first_tile[owner * blocks + inner] = (m - me_doc) * blocks
-        return carry
-
-    lax.fori_loop(0, n_doc, fill, 0)
-
+        if relay and k == 3:
+            relay_copy().wait_send()
+        else:
+            count_copy(k).wait_send()
+
+
+def place_kernel(tile_ref, tiles_ref, out_ref, sem):
     def step(row, carry):
-        tile = first_tile[pairs_ref[1, row]] + pairs_ref[0, row]
-        tile = jnp.where(row < count, tile, zero_tile)
+        tile = tile_ref[0, row]
         pltpu.make_async_copy(tiles_ref.at[tile], out_ref.at[row], sem).start()
         return carry
 
@@ -397,16 +432,21 @@
     hbm = pl.BlockSpec(memory_space=pltpu.HBM)
     smem = pl.BlockSpec(memory_space=pltpu.SMEM)
     vmem = pl.BlockSpec(memory_space=pltpu.VMEM)
-    tiles = pl.pallas_call(
+    tiles, numbers = pl.pallas_call(
         functools.partial(tiles_kernel, sizes),
-        out_shape=pltpu.VMEM((n_pair * n_right * blocks + 1, part_rows, rows), jnp.float32),
-        in_specs=[hbm, hbm, hbm, hbm],
-        out_specs=vmem,
+        out_shape=(
+            pltpu.VMEM((n_pair * n_right * blocks + 1, part_rows, rows), jnp.float32),
+            pltpu.SMEM((1, pairs.shape[0]), jnp.int32),
+        ),
+        in_specs=[hbm] * 5 + [smem],
+        out_specs=(vmem, smem),
         scratch_shapes=[
             pltpu.VMEM((blocks, slots), jnp.int32),
             pltpu.VMEM((blocks, slots), jnp.int32),
             pltpu.VMEM((blocks, slots, rows, cols), jnp.int32),
             pltpu.VMEM((blocks, rows), jnp.int32),
+            pltpu.VMEM((2, pairs.shape[0]), jnp.int32),
+            pltpu.VMEM((1, pairs.shape[0]), jnp.int32),
             pltpu.VMEM((blocks, slots, rows, cols), jnp.bfloat16),
             pltpu.VMEM((n_doc, blocks + 1, table_rows, cols), jnp.float32),
             pltpu.VMEM((n_doc, per_core, slots, rows, cols), jnp.bfloat16),
@@ -425,7 +465,7 @@
             pltpu.VMEM((square_rows, rows), jnp.float32),
             pltpu.VMEM((n_right, blocks, part_rows, rows), jnp.float32),
             pltpu.VMEM((n_pair, n_right, blocks, part_rows, rows), jnp.float32),
-            dma((3 + blocks,)),
+            dma((5 + blocks,)),
             dma((n_doc,)),
             dma((n_doc,)),
             dma((n_doc,)),
@@ -440,15 +480,15 @@
         compiler_params=pltpu.CompilerParams(
             collective_id=0, has_side_effects=True, vmem_limit_bytes=48 * 1024 * 1024
         ),
-    )(*[pltpu.with_memory_space_constraint(x, pltpu.HBM) for x in (live_slots, block_ids, counts, lengths.reshape(blocks, rows))])
+    )(*[pltpu.with_memory_space_constraint(x, pltpu.HBM) for x in (live_slots, block_ids, counts, lengths.reshape(blocks, rows), pairs.T)], pair_count)
     return pl.pallas_call(
-        functools.partial(place_kernel, sizes, blocks),
+        place_kernel,
         out_shape=jax.ShapeDtypeStruct((pairs.shape[0], part_rows, rows), jnp.float32),
-        in_specs=[smem, smem, pl.BlockSpec(memory_space=pl.ANY)],
+        in_specs=[smem, pl.BlockSpec(memory_space=pl.ANY)],
         out_specs=hbm,
-        scratch_shapes=[pltpu.SMEM((n_doc * blocks,), jnp.int32), dma(())],
+        scratch_shapes=[dma(())],
         compiler_params=pltpu.CompilerParams(vmem_limit_bytes=48 * 1024 * 1024),
-    )(pairs.T, pair_count, tiles)
+    )(numbers, tiles)
 
 
 def solution(mesh):

time: 22.6 us -> 22.6 us (level)
  no operation moved by 1% of the time
where the time goes in v5:
time: 22.6 us; the launch traced here: 22.5 us
  Pallas kernels  21.8 us (96%)
  between operations  0.66 us (3%)
    pallas_call x1, Pallas kernels, shards(): pl.pallas_call(functools.partial(tiles_kernel, sizes), out_shape=(pltpu.V...  20.8 us
    pallas_call x1, Pallas kernels, shards(): pl.pallas_call(place_kernel, out_shape=jax.ShapeDtypeStruct((pairs.shape[...  0.95 us

profile of v5, /device:TPU:0, one launch (start us, length us, event | category | flops | bytes accessed | tf_op | source)
XLA Modules:
  0.0 22.5 jit_solution(7269423712921920293)
XLA Ops:
  0.7 20.8 %shard_map.64 = (f32[17,32,128]{2,1,0:T(8,128)S(1)}, s32[1,64]{1,0:T(1,128)S(4)}) custom-call(s32[2,4]{1,0:T(2,128)} %live_hbm.1, s32[2,4]{1,0:T(2,128)} %ids_hbm.1, s32[2,4,128,128]{3,2,1,0:T(8,128)} %counts_hbm.1, s32[2,128]{1,0:T(2,128)} %bitcast.2, s32[2,64]{1,0:T(2,128)} %bitcast.3, s32[1]{0:T(128)S(6)} %copy.7.limit_ref), custom_call_target="tpu_custom_call" | custom-call | tf_op jit(solution)/shard_map/pallas_call | solution.py:435
  21.5 1.0 %shard_map.65 = f32[64,32,128]{2,1,0:T(8,128)} custom-call(s32[1,64]{1,0:T(1,128)S(4)} %get-tuple-element.7.tile_ref, f32[17,32,128]{2,1,0:T(8,128)S(1)} %get-tuple-element.8.tiles_ref), custom_call_target="tpu_custom_call" | custom-call | tf_op jit(solution)/shard_map/pallas_call | solution.py:484

commit v6 on v5

--- a/solution.py
+++ b/solution.py
@@ -122,7 +122,7 @@
             device_id_type=MESH,
         )
 
-    relay = n_doc == 4
+    relay = False
     near = 1 + lax.rem(me_pair, 2)
     far = 3 - near
 
@@ -273,7 +273,7 @@
         squares = jnp.where(diagonal, squares, 0.0)
         square_own[pl.ds(place, 1)] = jnp.sum(squares, axis=0, keepdims=True)
 
-    def grams(m, right, right_ids):
+    def align(m, right_ids):
         for b in range(blocks):
             left_ids = small[0, b, slots : 2 * slots]
             for j in range(slots):
@@ -282,9 +282,11 @@
                     same = left_ids[i : i + 1] == right_ids[j : j + 1]
                     same = jnp.where(same, 1.0, 0.0).astype(jnp.bfloat16)
                     total = total + left_weight[b, i] * same
-                aligned[b * rows : (b + 1) * rows, j * cols : (j + 1) * cols] = total
+                aligned[m, b * rows : (b + 1) * rows, j * cols : (j + 1) * cols] = total
+
+    def grams(m, right):
         gram = lax.dot_general(
-            aligned[...],
+            aligned[m],
             jnp.concatenate([right[j] for j in range(slots)], axis=1),
             (((1,), (1,)), ((), ())),
             preferred_element_type=jnp.float32,
@@ -304,6 +306,20 @@
     left_squares = [
         weigh(lambda s, b=b: masked[b, s], left_weight.at[b], b) for b in range(blocks)
     ]
+    for i in range(per_core):
+        own = me_pair * per_core + i
+        align(i, small[0, own, slots : 2 * slots])
+        grams(i, left_weight.at[own])
+    if relay:
+        count_copy(near).wait_recv()
+        relay_copy().start()
+
+    def align_right(k, carry):
+        for i in range(per_core):
+            align(k * per_core + i, small[k, me_pair * per_core + i, slots : 2 * slots])
+        return carry
+
+    lax.fori_loop(1, n_doc, align_right, 0)
     for load in extra:
         load.wait()
     left = pairs_ref[0:1]
@@ -319,12 +335,6 @@
     number_copy = pltpu.make_async_copy(number_ref, tile_ref, load_sem.at[4 + blocks])
     number_copy.start()
 
-    if relay:
-        count_copy(near).wait_recv()
-        relay_copy().start()
-    for i in range(per_core):
-        own = me_pair * per_core + i
-        grams(i, left_weight.at[own], small[0, own, slots : 2 * slots])
     for b in range(blocks):
         keep_squares(left_squares[b], b)
     for i in range(per_core):
@@ -347,7 +357,7 @@
         for i in range(per_core):
             m = k * per_core + i
             squares = weigh(lambda s, i=i: right_counts[k, i, s], right_weight, blocks + m)
-            grams(m, right_weight, small[k, me_pair * per_core + i, slots : 2 * slots])
+            grams(m, right_weight)
             keep_squares(squares, blocks + m)
         return carry
 
@@ -452,7 +462,7 @@
             pltpu.VMEM((n_doc, per_core, slots, rows, cols), jnp.bfloat16),
             pltpu.VMEM((blocks, slots, rows, cols), jnp.bfloat16),
             pltpu.VMEM((slots, rows, cols), jnp.bfloat16),
-            pltpu.VMEM((blocks * rows, slots * cols), jnp.bfloat16),
+            pltpu.VMEM((n_right, blocks * rows, slots * cols), jnp.bfloat16),
             pltpu.VMEM(((blocks + n_right) * slots, cols), jnp.float32),
             pltpu.VMEM(((blocks + n_right) * slots, cols), jnp.float32),
             pltpu.VMEM((blocks + n_right, rows, rows), jnp.float32),

time: 22.6 us -> 21.8 us (0.965)
  Pallas kernels: 21.8 us -> 21 us
    pallas_call x1, Pallas kernels: 20.8 us -> 20 us  [shards(): pl.pallas_call(functools.partial(tiles_kernel, sizes), out_shape=(pltpu.V...]
where the time goes in v6:
time: 21.8 us; the launch traced here: 21.6 us
  Pallas kernels  21 us (96%)
  between operations  0.66 us (3%)
    pallas_call x1, Pallas kernels, shards(): pl.pallas_call(functools.partial(tiles_kernel, sizes), out_shape=(pltpu.V...  20 us
    pallas_call x1, Pallas kernels, shards(): pl.pallas_call(place_kernel, out_shape=jax.ShapeDtypeStruct((pairs.shape[...  0.95 us

profile of v6, /device:TPU:0, one launch (start us, length us, event | category | flops | bytes accessed | tf_op | source)
XLA Modules:
  0.0 21.6 jit_solution(7386524326778011273)
XLA Ops:
  0.7 20.0 %shard_map.64 = (f32[17,32,128]{2,1,0:T(8,128)S(1)}, s32[1,64]{1,0:T(1,128)S(4)}) custom-call(s32[2,4]{1,0:T(2,128)} %live_hbm.1, s32[2,4]{1,0:T(2,128)} %ids_hbm.1, s32[2,4,128,128]{3,2,1,0:T(8,128)} %counts_hbm.1, s32[2,128]{1,0:T(2,128)} %bitcast.2, s32[2,64]{1,0:T(2,128)} %bitcast.3, s32[1]{0:T(128)S(6)} %copy.7.limit_ref), custom_call_target="tpu_custom_call" | custom-call | tf_op jit(solution)/shard_map/pallas_call | solution.py:445
  20.7 1.0 %shard_map.65 = f32[64,32,128]{2,1,0:T(8,128)} custom-call(s32[1,64]{1,0:T(1,128)S(4)} %get-tuple-element.7.tile_ref, f32[17,32,128]{2,1,0:T(8,128)S(1)} %get-tuple-element.8.tiles_ref), custom_call_target="tpu_custom_call" | custom-call | tf_op jit(solution)/shard_map/pallas_call | solution.py:494

commit v7 on v6

--- a/solution.py
+++ b/solution.py
@@ -122,20 +122,6 @@
             device_id_type=MESH,
         )
 
-    relay = False
-    near = 1 + lax.rem(me_pair, 2)
-    far = 3 - near
-
-    def relay_copy():
-        return pltpu.make_async_remote_copy(
-            src_ref=right_counts.at[near],
-            dst_ref=right_counts.at[3],
-            send_sem=count_send_sem.at[3],
-            recv_sem=count_recv_sem.at[3],
-            device_id=doc_peer(far),
-            device_id_type=MESH,
-        )
-
     def term_copy(m, k):
         return pltpu.make_async_remote_copy(
             src_ref=coded.at[m, lax.rem(me_term + k, n_term)],
@@ -209,7 +195,8 @@
 
     for k in range(1, n_doc):
         small_copy(k).start()
-    for k in (near, far) if relay else range(1, n_doc):
+    first = [k for k in range(1, n_doc) if k & (k - 1) == 0]
+    for k in first:
         count_copy(k).start()
     for k in range(1, n_doc):
         small_copy(k).wait_recv()
@@ -306,13 +293,13 @@
     left_squares = [
         weigh(lambda s, b=b: masked[b, s], left_weight.at[b], b) for b in range(blocks)
     ]
+    for k in range(1, n_doc):
+        if k not in first:
+            count_copy(k).start()
     for i in range(per_core):
         own = me_pair * per_core + i
         align(i, small[0, own, slots : 2 * slots])
         grams(i, left_weight.at[own])
-    if relay:
-        count_copy(near).wait_recv()
-        relay_copy().start()
 
     def align_right(k, carry):
         for i in range(per_core):
@@ -340,20 +327,8 @@
     for i in range(per_core):
         square_own[pl.ds(blocks + i, 1)] = square_own[pl.ds(me_pair * per_core + i, 1)]
 
-    def right_step(step, carry):
-        if relay:
-            k = jnp.where(step == 1, near, jnp.where(step == 2, far, 3))
-
-            @pl.when(step == 2)
-            def _():
-                count_copy(far).wait_recv()
-
-            @pl.when(step == 3)
-            def _():
-                relay_copy().wait_recv()
-        else:
-            k = step
-            count_copy(k).wait_recv()
+    def right_step(k, carry):
+        count_copy(k).wait_recv()
         for i in range(per_core):
             m = k * per_core + i
             squares = weigh(lambda s, i=i: right_counts[k, i, s], right_weight, blocks + m)
@@ -413,10 +388,7 @@
         side_copy(k).wait_send()
     for k in range(1, n_doc):
         small_copy(k).wait_send()
-        if relay and k == 3:
-            relay_copy().wait_send()
-        else:
-            count_copy(k).wait_send()
+        count_copy(k).wait_send()
 
 
 def place_kernel(tile_ref, tiles_ref, out_ref, sem):

time: 21.8 us -> 21.9 us (level)
  no operation moved by 1% of the time
where the time goes in v7:
time: 21.9 us; the launch traced here: 21.8 us
  Pallas kernels  21.1 us (96%)
  between operations  0.66 us (3%)
    pallas_call x1, Pallas kernels, shards(): pl.pallas_call(functools.partial(tiles_kernel, sizes), out_shape=(pltpu.V...  20.1 us
    pallas_call x1, Pallas kernels, shards(): pl.pallas_call(place_kernel, out_shape=jax.ShapeDtypeStruct((pairs.shape[...  0.95 us

profile of v7, /device:TPU:0, one launch (start us, length us, event | category | flops | bytes accessed | tf_op | source)
XLA Modules:
  0.0 21.8 jit_solution(8797931490307372231)
XLA Ops:
  0.7 20.1 %shard_map.64 = (f32[17,32,128]{2,1,0:T(8,128)S(1)}, s32[1,64]{1,0:T(1,128)S(4)}) custom-call(s32[2,4]{1,0:T(2,128)} %live_hbm.1, s32[2,4]{1,0:T(2,128)} %ids_hbm.1, s32[2,4,128,128]{3,2,1,0:T(8,128)} %counts_hbm.1, s32[2,128]{1,0:T(2,128)} %bitcast.2, s32[2,64]{1,0:T(2,128)} %bitcast.3, s32[1]{0:T(128)S(6)} %copy.7.limit_ref), custom_call_target="tpu_custom_call" | custom-call | tf_op jit(solution)/shard_map/pallas_call | solution.py:417
  20.8 1.0 %shard_map.65 = f32[64,32,128]{2,1,0:T(8,128)} custom-call(s32[1,64]{1,0:T(1,128)S(4)} %get-tuple-element.7.tile_ref, f32[17,32,128]{2,1,0:T(8,128)S(1)} %get-tuple-element.8.tiles_ref), custom_call_target="tpu_custom_call" | custom-call | tf_op jit(solution)/shard_map/pallas_call | solution.py:466

commit v8 on v7

--- a/solution.py
+++ b/solution.py
@@ -97,7 +97,7 @@
         return {"doc": target_of(me_doc, k, n_doc)}
 
     def term_peer(k):
-        return {"term": lax.rem(me_term + k, n_term)}
+        return {"term": target_of(me_term, k, n_term)}
 
     def pair_peer(k):
         return {"pair": lax.rem(me_pair + k, n_pair)}
@@ -124,7 +124,7 @@
 
     def term_copy(m, k):
         return pltpu.make_async_remote_copy(
-            src_ref=coded.at[m, lax.rem(me_term + k, n_term)],
+            src_ref=coded.at[m, target_of(me_term, k, n_term)],
             dst_ref=term_recv.at[m, k],
             send_sem=term_send_sem.at[m, k],
             recv_sem=term_recv_sem.at[m, k],
@@ -134,7 +134,7 @@
 
     def side_copy(k):
         return pltpu.make_async_remote_copy(
-            src_ref=side_own.at[lax.rem(me_term + k, n_term)],
+            src_ref=side_own.at[target_of(me_term, k, n_term)],
             dst_ref=side_recv.at[k],
             send_sem=side_send_sem.at[k],
             recv_sem=side_recv_sem.at[k],
@@ -195,8 +195,7 @@
 
     for k in range(1, n_doc):
         small_copy(k).start()
-    first = [k for k in range(1, n_doc) if k & (k - 1) == 0]
-    for k in first:
+    for k in sorted(range(1, n_doc), key=lambda k: k & (k - 1) != 0):
         count_copy(k).start()
     for k in range(1, n_doc):
         small_copy(k).wait_recv()
@@ -287,15 +286,12 @@
                 code = (piece * (steps / top) + 0.5).astype(jnp.int32)
                 coded[m, z, b] = code.astype(jnp.int16)
                 side_own[z, pl.ds(m * blocks + b, 1)] = top * (1.0 / steps)
-        for k in range(1, n_term):
+        for k in reversed(range(1, n_term)):
             term_copy(m, k).start()
 
     left_squares = [
         weigh(lambda s, b=b: masked[b, s], left_weight.at[b], b) for b in range(blocks)
     ]
-    for k in range(1, n_doc):
-        if k not in first:
-            count_copy(k).start()
     for i in range(per_core):
         own = me_pair * per_core + i
         align(i, small[0, own, slots : 2 * slots])
@@ -342,7 +338,7 @@
     squares = square_own[...]
     for z in range(n_term):
         side_own[z, scale_rows:] = squares
-    for k in range(1, n_term):
+    for k in reversed(range(1, n_term)):
         side_copy(k).start()
     for k in range(1, n_term):
         side_copy(k).wait_recv()

time: 21.9 us -> 21.8 us (level)
  no operation moved by 1% of the time
where the time goes in v8:
time: 21.8 us; the launch traced here: 21.6 us
  Pallas kernels  21 us (96%)
  between operations  0.66 us (3%)
    pallas_call x1, Pallas kernels, shards(): pl.pallas_call(functools.partial(tiles_kernel, sizes), out_shape=(pltpu.V...  20 us
    pallas_call x1, Pallas kernels, shards(): pl.pallas_call(place_kernel, out_shape=jax.ShapeDtypeStruct((pairs.shape[...  0.95 us

profile of v8, /device:TPU:0, one launch (start us, length us, event | category | flops | bytes accessed | tf_op | source)
XLA Modules:
  0.0 21.6 jit_solution(13175236073007414779)
XLA Ops:
  0.7 20.0 %shard_map.64 = (f32[17,32,128]{2,1,0:T(8,128)S(1)}, s32[1,64]{1,0:T(1,128)S(4)}) custom-call(s32[2,4]{1,0:T(2,128)} %live_hbm.1, s32[2,4]{1,0:T(2,128)} %ids_hbm.1, s32[2,4,128,128]{3,2,1,0:T(8,128)} %counts_hbm.1, s32[2,128]{1,0:T(2,128)} %bitcast.2, s32[2,64]{1,0:T(2,128)} %bitcast.3, s32[1]{0:T(128)S(6)} %copy.7.limit_ref), custom_call_target="tpu_custom_call" | custom-call | tf_op jit(solution)/shard_map/pallas_call | solution.py:413
  20.7 1.0 %shard_map.65 = f32[64,32,128]{2,1,0:T(8,128)} custom-call(s32[1,64]{1,0:T(1,128)S(4)} %get-tuple-element.7.tile_ref, f32[17,32,128]{2,1,0:T(8,128)S(1)} %get-tuple-element.8.tiles_ref), custom_call_target="tpu_custom_call" | custom-call | tf_op jit(solution)/shard_map/pallas_call | solution.py:462

commit v9 on v6

--- a/solution.py
+++ b/solution.py
@@ -395,7 +395,7 @@
             pair_copy(m, k).start()
         return carry
 
-    lax.fori_loop(0, n_right, finish, 0)
+    lax.fori_loop(0, n_right, finish, 0, unroll=min(n_right, 4))
 
     def collect(m, carry):
         for k in range(1, n_pair):
@@ -407,7 +407,7 @@
             pair_copy(m, k).wait_send()
         return carry
 
-    lax.fori_loop(0, n_right, collect, 0)
+    lax.fori_loop(0, n_right, collect, 0, unroll=min(n_right, 4))
     number_copy.wait()
     for k in range(1, n_term):
         side_copy(k).wait_send()

time: 21.8 us -> 21.8 us (level)
  no operation moved by 1% of the time
where the time goes in v9:
time: 21.8 us; the launch traced here: 21.6 us
  Pallas kernels  21 us (96%)
  between operations  0.66 us (3%)
    pallas_call x1, Pallas kernels, shards(): pl.pallas_call(functools.partial(tiles_kernel, sizes), out_shape=(pltpu.V...  20 us
    pallas_call x1, Pallas kernels, shards(): pl.pallas_call(place_kernel, out_shape=jax.ShapeDtypeStruct((pairs.shape[...  0.95 us

profile of v9, /device:TPU:0, one launch (start us, length us, event | category | flops | bytes accessed | tf_op | source)
XLA Modules:
  0.0 21.6 jit_solution(4918185500370952704)
XLA Ops:
  0.7 20.0 %shard_map.64 = (f32[17,32,128]{2,1,0:T(8,128)S(1)}, s32[1,64]{1,0:T(1,128)S(4)}) custom-call(s32[2,4]{1,0:T(2,128)} %live_hbm.1, s32[2,4]{1,0:T(2,128)} %ids_hbm.1, s32[2,4,128,128]{3,2,1,0:T(8,128)} %counts_hbm.1, s32[2,128]{1,0:T(2,128)} %bitcast.2, s32[2,64]{1,0:T(2,128)} %bitcast.3, s32[1]{0:T(128)S(6)} %copy.7.limit_ref), custom_call_target="tpu_custom_call" | custom-call | tf_op jit(solution)/shard_map/pallas_call | solution.py:445
  20.7 1.0 %shard_map.65 = f32[64,32,128]{2,1,0:T(8,128)} custom-call(s32[1,64]{1,0:T(1,128)S(4)} %get-tuple-element.7.tile_ref, f32[17,32,128]{2,1,0:T(8,128)S(1)} %get-tuple-element.8.tiles_ref), custom_call_target="tpu_custom_call" | custom-call | tf_op jit(solution)/shard_map/pallas_call | solution.py:494
